TPU v7x, 256 devices: a whole 4x4x8 slice. The times are simulated.
256 devices in a mesh: rows: 64 (over x, z, core), cols: 4 (over y).
Axes of the slice: x: 4, y: 4, z: 8, core: 2. Of those that a mesh axis runs over, the one named last changes fastest.
Arguments:
- kernel: float32 [16384, 16384], P('rows', 'cols'), may hold values from 0 to 2, as said below
- row_block: int32 [256], P('rows'), may hold values from 0 to 255, as said below
- panel_order: int32 [2], replicated, may hold values from 0 to 63, as said below
- samples: float32 [16384, 512], P('rows', 'cols'), may hold values from -6 to 6
Outputs:
- trailing: float32 [16384, 16384], P('rows', 'cols')
- factor: float32 [16384, 512], P('rows')
- solved: float32 [512, 512], P(None, 'cols')
- reduced_samples: float32 [16384, 512], P('rows', 'cols')
Inputs may be any that keep to these rules, and one draw needn't show every extreme that they name: `row_block`: the stored row blocks of rows index i (stored blocks i * 4 to (i + 1) * 4 - 1) hold the global row blocks i + t * 64, t = 0 .. 3, each once, in some order. `panel_order`: the entries are distinct, and one of them is 63. `kernel`: in global row order the matrix is symmetric and positive definite, its smallest eigenvalue 0.25 or more.
All inputs are finite; a program needn't handle non-finite values.
Results may differ from a plain program's by a relative error of at most 0.0003.
Values sent between devices are 32-bit elements; how exact they have to be, the bound alone decides.
No kernel may reach another device: no remote copies, remote signals or barrier semaphores. Data moves between devices by JAX's collectives and lax.ppermute only.
A program may use at most 128 MiB of HBM per device.

v0:
```python
import jax
import jax.numpy as jnp
from jax import lax
from jax.experimental import pallas as pl
from jax.experimental.pallas import tpu as pltpu
from jax.sharding import PartitionSpec as P

PW = 256
PANELS = 2
EXACT = lax.Precision.HIGHEST
SIDE = 128
STEP = 8


def dot_nt(a, b, precision=EXACT):
    return lax.dot_general(a, b, (((1,), (1,)), ((), ())), precision=precision, preferred_element_type=jnp.float32)


def dot_nn(a, b, precision=EXACT):
    return lax.dot_general(a, b, (((1,), (0,)), ((), ())), precision=precision, preferred_element_type=jnp.float32)


def lanes_of(rows, lane):
    return jnp.broadcast_to(rows[:, lane : lane + 1], (STEP, SIDE))


def sublanes_of(rows, sub):
    return jnp.broadcast_to(rows[sub : sub + 1, :], (STEP, SIDE))


def small_inverse(spread):
    inv, low = [None] * STEP, [[None] * STEP for _ in range(STEP)]
    rest = [list(r) for r in spread]
    for s in range(STEP):
        inv[s] = lax.rsqrt(rest[s][s])
        for r in range(s + 1, STEP):
            low[r][s] = rest[r][s] * inv[s]
        for r in range(s + 1, STEP):
            for q in range(s + 1, r + 1):
                rest[r][q] = rest[r][q] - low[r][s] * low[q][s]
    out = [[None] * STEP for _ in range(STEP)]
    for r in range(STEP):
        out[r][r] = inv[r]
        for s in range(r):
            total = low[r][s] * out[s][s]
            for q in range(s + 1, r):
                total = total + low[r][q] * out[q][s]
            out[r][s] = -inv[r] * total
    return out


def tile_inverse(d_ref, x_ref):
    groups = SIDE // STEP
    sub = lax.broadcasted_iota(jnp.int32, (STEP, SIDE), 0)
    lane = lax.broadcasted_iota(jnp.int32, (STEP, SIDE), 1)
    left = [d_ref[STEP * g : STEP * (g + 1), :] for g in range(groups)]
    right = [jnp.where(lane == sub + STEP * g, 1.0, 0.0).astype(jnp.float32) for g in range(groups)]
    for b in range(groups):
        here_l, here_r = left[b], right[b]
        cols = [lanes_of(here_l, STEP * b + s) for s in range(STEP)]
        spread = [[sublanes_of(cols[s], r) if s <= r else None for s in range(STEP)] for r in range(STEP)]
        v = small_inverse(spread)
        in_l = [sublanes_of(here_l, s) for s in range(STEP)]
        in_r = [sublanes_of(here_r, s) for s in range(STEP)]
        out_l, out_r = [], []
        for r in range(STEP):
            tl, tr = v[r][0] * in_l[0], v[r][0] * in_r[0]
            for s in range(1, r + 1):
                tl, tr = tl + v[r][s] * in_l[s], tr + v[r][s] * in_r[s]
            out_l.append(tl)
            out_r.append(tr)
        new_r = out_r[0]
        for r in range(1, STEP):
            new_r = jnp.where(sub == r, out_r[r], new_r)
        x_ref[STEP * b : STEP * (b + 1), :] = new_r
        if b + 1 == groups:
            break
        t_l, t_r = [], []
        for s in range(STEP):
            tl, tr = v[STEP - 1][s] * out_l[STEP - 1], v[STEP - 1][s] * out_r[STEP - 1]
            for r in range(s, STEP - 1):
                tl, tr = tl + v[r][s] * out_l[r], tr + v[r][s] * out_r[r]
            t_l.append(tl)
            t_r.append(tr)
        for g in range(b + 1, groups):
            c = [lanes_of(left[g], STEP * b + s) for s in range(STEP)]
            sl, sr = c[0] * t_l[0], c[0] * t_r[0]
            for s in range(1, STEP):
                sl, sr = sl + c[s] * t_l[s], sr + c[s] * t_r[s]
            left[g], right[g] = left[g] - sl, right[g] - sr


def halves(array):
    high = array.astype(jnp.bfloat16)
    return high, (array - high.astype(jnp.float32)).astype(jnp.bfloat16)


def two_tiles(a, v, d, x):
    v[...] = jnp.zeros_like(v)

    @pl.loop(0, 2)
    def _(k):
        at = pl.multiple_of(k * SIDE, SIDE)
        d[...] = a[pl.ds(at, SIDE), pl.ds(at, SIDE)]
        tile_inverse(d, x)

        @pl.when(k == 0)
        def _():
            own = x[...]
            v[:SIDE, :SIDE] = own
            below = dot_nt(a[SIDE:, :SIDE], own)
            a[SIDE:, SIDE:] = a[SIDE:, SIDE:] - dot_nt(below, below)
            v[SIDE:, :SIDE] = -dot_nn(below, own)

        @pl.when(k == 1)
        def _():
            own = x[...]
            v[SIDE:, SIDE:] = own
            v[SIDE:, :SIDE] = dot_nn(own, v[SIDE:, :SIDE])


def first_kernel(own_ref, other_ref, v_ref, rest_ref, under_ref, right_ref, a, top, d, x):
    row_place, col_place = lax.axis_index("rows"), lax.axis_index("cols")
    core, odd = row_place & 1, (row_place >> 1) & 1
    strata = lax.axis_size("cols")
    share = own_ref.shape[0] // (strata + 1)
    part_rows = share // (2 * PANELS)
    block_rows = part_rows * strata
    for c, source in enumerate((own_ref, other_ref)):
        for z in range(2):
            member = (odd ^ z) * 2 + (core ^ c)
            for k in range(PANELS):
                base = k * PW + member * block_rows
                lo = (z * PANELS + k) * part_rows
                for shift in range(strata):
                    part = (col_place - shift) & (strata - 1)
                    at = pl.multiple_of(base + part * part_rows, part_rows)
                    a[pl.ds(at, part_rows), :] = source[shift * share + lo : shift * share + lo + part_rows, :]
                for chunk in range(block_rows // part_rows):
                    at = pl.multiple_of(base + chunk * part_rows, part_rows)
                    right_ref[pl.ds(at, part_rows), :] = source[
                        strata * share + lo : strata * share + lo + part_rows, chunk * SIDE : (chunk + 1) * SIDE
                    ]
    top[...] = a[:PW, :PW]
    two_tiles(top, v_ref, d, x)
    v = v_ref[...]
    low = dot_nt(a[PW:, :PW], v)
    rest_ref[...] = a[PW:, PW:] - dot_nt(low, low)
    under_ref[...] = -dot_nn(low, v)


def square(side):
    return jax.ShapeDtypeStruct((side, side), jnp.float32)


def first_call(own, other):
    right = jax.ShapeDtypeStruct((PANELS * PW, SIDE), jnp.float32)
    return pl.pallas_call(
        first_kernel,
        out_shape=[square(PW), square(PW), square(PW), right],
        scratch_shapes=[
            pltpu.VMEM((PANELS * PW, PANELS * PW), jnp.float32),
            pltpu.VMEM((PW, PW), jnp.float32),
            pltpu.VMEM((SIDE, SIDE), jnp.float32),
            pltpu.VMEM((SIDE, SIDE), jnp.float32),
        ],
        cost_estimate=pl.CostEstimate(flops=12_000_000_000, bytes_accessed=2_000_000, transcendentals=0),
        compiler_params=pltpu.CompilerParams(vmem_limit_bytes=16 * 1024 * 1024),
        name="eliminate_first",
    )(own, other)


def second_kernel(rest_ref, under_ref, v_ref, cross_ref, a, d, x):
    a[...] = rest_ref[...]
    two_tiles(a, v_ref, d, x)
    cross_ref[...] = dot_nn(v_ref[...], under_ref[...])


def second_call(rest, under):
    return pl.pallas_call(
        second_kernel,
        out_shape=[square(PW), square(PW)],
        scratch_shapes=[
            pltpu.VMEM((PW, PW), jnp.float32),
            pltpu.VMEM((SIDE, SIDE), jnp.float32),
            pltpu.VMEM((SIDE, SIDE), jnp.float32),
        ],
        cost_estimate=pl.CostEstimate(flops=12_000_000_000, bytes_accessed=2_000_000, transcendentals=0),
        compiler_params=pltpu.CompilerParams(vmem_limit_bytes=16 * 1024 * 1024),
        name="eliminate_second",
    )(rest, under)


def apply_kernel(block_ref, *refs):
    pieces, (v1_ref, cross_ref, v2_ref, rc_ref, ri_ref, f_ref, w_ref, y_ref, r_ref, p) = refs[:-10], refs[-10:]
    me = lax.axis_index("cols")
    rows_count = lax.axis_size("rows")
    block_rows = pieces[0].shape[0]
    for u in range(len(pieces)):
        shift = (me - lax.div(block_ref[u], rows_count)) & (len(pieces) - 1)
        for s, piece in enumerate(pieces):

            @pl.when(shift == s)
            def _():
                p[u * block_rows : (u + 1) * block_rows] = piece[...]

    v1, cross, v2 = v1_ref[...], cross_ref[...], v2_ref[...]
    p1, p2 = p[:, :PW], p[:, PW:]
    f1 = dot_nt(p1, v1)
    f2 = dot_nt(p1, cross) + dot_nt(p2, v2)
    f_ref[:, :PW] = f1
    f_ref[:, PW:] = f2
    w_ref[:, :PW] = dot_nn(f1, v1) + dot_nn(f2, cross)
    w_ref[:, PW:] = dot_nn(f2, v2)
    y1 = dot_nn(v1, rc_ref[:PW])
    y2 = dot_nn(cross, rc_ref[:PW]) + dot_nn(v2, rc_ref[PW:])
    y_ref[:PW] = y1
    y_ref[PW:] = y2
    r_ref[...] = ri_ref[...] - dot_nn(f1, y1) - dot_nn(f2, y2)


def apply_call(row_block, pieces, v1, cross, v2, rc, ri):
    size, right = rc.shape
    rows = ri.shape[0]
    f32 = jnp.float32
    operands = (*pieces, v1, cross, v2, rc, ri)
    return pl.pallas_call(
        apply_kernel,
        in_specs=[pl.BlockSpec(memory_space=pltpu.SMEM)]
        + [pl.BlockSpec(memory_space=pltpu.VMEM)] * len(operands),
        out_shape=[
            jax.ShapeDtypeStruct((rows, size), f32),
            jax.ShapeDtypeStruct((rows, size), f32),
            jax.ShapeDtypeStruct((size, right), f32),
            jax.ShapeDtypeStruct((rows, right), f32),
        ],
        scratch_shapes=[pltpu.VMEM((rows, size), f32)],
        cost_estimate=pl.CostEstimate(flops=4_000_000_000, bytes_accessed=4_000_000, transcendentals=0),
        compiler_params=pltpu.CompilerParams(vmem_limit_bytes=16 * 1024 * 1024),
        name="apply_factor",
    )(row_block, *operands)


WIDTH = 512


def update_kernel(k_ref, w_ref, b_ref, o_ref, held, gathered, out, k_sems, b_sems, out_sems):
    cols = k_ref.shape[1]
    parts = [slice(i * WIDTH, (i + 1) * WIDTH) for i in range(cols // WIDTH)]
    b_loads = [pltpu.make_async_copy(b_ref.at[at], gathered.at[at], b_sems.at[i]) for i, at in enumerate(parts)]
    k_loads = [pltpu.make_async_copy(k_ref.at[:, at], held.at[:, at], k_sems.at[i]) for i, at in enumerate(parts)]
    for b_load, k_load in zip(b_loads, k_loads):
        b_load.start()
        k_load.start()
    wh, wl = halves(w_ref[...])
    stores = []
    for i, at in enumerate(parts):
        b_loads[i].wait()
        top, bottom = halves(gathered[at])
        total = dot_nt(wh, top, None) + dot_nt(wh, bottom, None) + dot_nt(wl, top, None)
        k_loads[i].wait()
        out[:, at] = held[:, at] - total
        stores.append(pltpu.make_async_copy(out.at[:, at], o_ref.at[:, at], out_sems.at[i]))
        stores[-1].start()
    for store in stores:
        store.wait()


def update_call(kernel, weights, across):
    rows, cols = kernel.shape
    size = weights.shape[1]
    count = cols // WIDTH
    f32 = jnp.float32
    return pl.pallas_call(
        update_kernel,
        in_specs=[
            pl.BlockSpec(memory_space=pltpu.HBM),
            pl.BlockSpec(memory_space=pltpu.VMEM),
            pl.BlockSpec(memory_space=pltpu.HBM),
        ],
        out_specs=pl.BlockSpec(memory_space=pltpu.HBM),
        out_shape=jax.ShapeDtypeStruct((rows, cols), f32),
        scratch_shapes=[
            pltpu.VMEM((rows, cols), f32),
            pltpu.VMEM((cols, size), f32),
            pltpu.VMEM((rows, cols), f32),
            pltpu.SemaphoreType.DMA((count,)),
            pltpu.SemaphoreType.DMA((count,)),
            pltpu.SemaphoreType.DMA((count,)),
        ],
        cost_estimate=pl.CostEstimate(flops=6 * rows * cols * size, bytes_accessed=16_000_000, transcendentals=0),
        compiler_params=pltpu.CompilerParams(vmem_limit_bytes=54 * 1024 * 1024),
        name="trailing_update",
    )(kernel, weights, across)


def pack_kernel(order_ref, block_ref, kernel_ref, samples_ref, *rest):
    messages, right_ref, masks, own, sems = rest[:-5], rest[-5], rest[-4:-2], rest[-2], rest[-1]
    strata = len(messages) // 2
    me = lax.axis_index("cols")
    local_cols = kernel_ref.shape[1]
    blocks_here = strata
    block_rows = kernel_ref.shape[0] // blocks_here
    part_rows = block_rows // strata
    per_place = local_cols // PW
    copies = []
    for k in range(PANELS):
        at = pl.multiple_of(lax.rem(order_ref[k], per_place) * PW, PW)
        copies.append(
            pltpu.make_async_copy(
                kernel_ref.at[:, pl.ds(at, PW)], own.at[:, k * PW : (k + 1) * PW], sems.at[k]
            )
        )
        copies[-1].start()
    rows_count = lax.axis_size("rows")

    def start_of(stratum):
        slot = jnp.int32(0)
        for u in range(blocks_here):
            slot = jnp.where(lax.div(block_ref[u], rows_count) == stratum, u, slot)
        return slot * block_rows

    starts = [start_of(lax.div(order_ref[k], per_place)) for k in range(PANELS)]
    for k in range(PANELS):
        right_ref[k] = samples_ref[pl.ds(pl.multiple_of(starts[k], block_rows), block_rows), :]
    z_here = (lax.axis_index("rows") >> 2) & 3
    for k in range(PANELS):
        z_at = lax.rem(order_ref[k], 4)
        rows = slice(k * 2 * part_rows, (k + 1) * 2 * part_rows)
        swaps = (z_at == (z_here ^ 1), (z_at >> 1) != (z_here >> 1))
        for mask, swap in zip(masks, swaps):
            mask[rows] = jnp.full((2 * part_rows, mask.shape[1]), jnp.where(swap, 1, 0), jnp.int32)
    for copy in copies:
        copy.wait()
    for shift in range(strata):
        to = (me + shift) & (strata - 1)
        out, share = messages[shift], messages[strata + shift]
        out[...] = own[pl.ds(pl.multiple_of(start_of(to), block_rows), block_rows), :]
        for k in range(PANELS):
            lo = k * part_rows
            at = pl.multiple_of(starts[k] + to * part_rows, part_rows)
            share[lo : lo + part_rows] = own[pl.ds(at, part_rows), :]


def pack_call(panel_order, row_block, kernel, samples):
    strata = lax.axis_size("cols")
    rows, right = samples.shape
    block_rows = rows // row_block.shape[0]
    size = PANELS * PW
    f32 = jnp.float32
    message = pltpu.VMEM((block_rows, size), f32)
    share = pltpu.VMEM((PANELS * (block_rows // strata), size), f32)
    mask = pltpu.VMEM((PANELS * 2 * (block_rows // strata), size), jnp.int32)
    *messages, picked, first, second = pl.pallas_call(
        pack_kernel,
        in_specs=[
            pl.BlockSpec(memory_space=pltpu.SMEM),
            pl.BlockSpec(memory_space=pltpu.SMEM),
            pl.BlockSpec(memory_space=pltpu.HBM),
            pl.BlockSpec(memory_space=pltpu.VMEM),
        ],
        out_shape=[message] * strata
        + [share] * strata
        + [pltpu.VMEM((PANELS, block_rows, right), f32), mask, mask],
        scratch_shapes=[pltpu.VMEM((rows, size), f32), pltpu.SemaphoreType.DMA((PANELS,))],
        cost_estimate=pl.CostEstimate(flops=0, bytes_accessed=2_000_000, transcendentals=0),
        compiler_params=pltpu.CompilerParams(vmem_limit_bytes=60 * 1024 * 1024),
        name="pack_messages",
    )(panel_order, row_block, kernel, samples)
    return messages[:strata], messages[strata:], picked, (first, second)


def shift_of(order_ref, k, axis, strata):
    per_place = lax.axis_size("rows") // strata
    if axis == "cols":
        return (lax.axis_index("cols") - lax.div(order_ref[k], per_place)) & (strata - 1)
    return ((lax.axis_index("rows") >> 4) - lax.div(lax.rem(order_ref[k], per_place), 4)) & 3


def piece_kernel(order_ref, *refs):
    got, out_ref = refs[:-1], refs[-1]
    for k in range(PANELS):
        columns = slice(k * PW, (k + 1) * PW)
        shift = shift_of(order_ref, k, "cols", len(got))
        for s, source in enumerate(got):

            @pl.when(shift == s)
            def _():
                out_ref[:, columns] = source[:, columns]


def share_kernel(order_ref, *refs):
    got, (right_ref, out_ref) = refs[:-2], refs[-2:]
    part_rows = right_ref.shape[1] // len(got)
    for k in range(PANELS):
        columns = slice(k * PW, (k + 1) * PW)
        lo = (2 * k + 1) * part_rows
        for chunk in range(len(got)):
            out_ref[lo : lo + part_rows, chunk * SIDE : (chunk + 1) * SIDE] = right_ref[
                k, chunk * part_rows : (chunk + 1) * part_rows
            ]
        shift = shift_of(order_ref, k, "cols", len(got))
        for s, source in enumerate(got):

            @pl.when(shift == s)
            def _():
                for p in range(PANELS):
                    out_ref[2 * p * part_rows : (2 * p + 1) * part_rows, columns] = source[
                        p * part_rows : (p + 1) * part_rows, columns
                    ]


def load_kernel(order_ref, *refs):
    got, out_ref = refs[:-1], refs[-1]
    rows = out_ref.shape[0] // PANELS
    for k in range(PANELS):
        at = slice(k * rows, (k + 1) * rows)
        shift = shift_of(order_ref, k, "rows", lax.axis_size("cols"))
        for s, source in enumerate(got):

            @pl.when(shift == s)
            def _():
                out_ref[at] = source[at]


def choose_call(body, panel_order, got, rows, name):
    return pl.pallas_call(
        body,
        in_specs=[pl.BlockSpec(memory_space=pltpu.SMEM)] + [pl.BlockSpec(memory_space=pltpu.VMEM)] * len(got),
        out_shape=jax.ShapeDtypeStruct((rows, PANELS * PW), jnp.float32),
        cost_estimate=pl.CostEstimate(flops=0, bytes_accessed=1_000_000, transcendentals=0),
        compiler_params=pltpu.CompilerParams(vmem_limit_bytes=16 * 1024 * 1024),
        name=name,
    )(panel_order, *got)


def on_device(kernel, row_block, panel_order, samples):
    rows_count, cols_count = lax.axis_size("rows"), lax.axis_size("cols")
    block_rows = kernel.shape[0] // row_block.shape[0]
    part_rows = block_rows // cols_count

    def along_y(array, shift):
        return lax.ppermute(
            array, "cols", [(i, (i + shift) % cols_count) for i in range(cols_count)]
        )

    def along_rows(array, move):
        pairs = []
        for r in range(rows_count):
            x, z, core = move(r // 16, r % 16 // 2, r % 2)
            pairs.append((r, x % 4 * 16 + z % 8 * 2 + core))
        return lax.ppermute(array, "rows", pairs)

    def along_x(array, shift):
        return along_rows(array, lambda x, z, c: (x + shift, z, c))

    def to_core(array):
        return along_rows(array, lambda x, z, c: (x, z, c ^ 1))

    messages, shares, right, masks = pack_call(panel_order, row_block, kernel, samples)
    got = messages[:1] + [along_y(messages[s], s) for s in range(1, cols_count)]
    piece = choose_call(piece_kernel, panel_order, got, block_rows, "choose_pieces")
    across = lax.all_gather(piece, "rows", axis=0, tiled=True)
    got = shares[:1] + [along_y(shares[s], s) for s in range(1, cols_count)]
    load = choose_call(share_kernel, panel_order, [*got, right], block_rows, "choose_shares")

    got = [load] + [along_x(load, s) for s in range(1, 4)]
    load = choose_call(load_kernel, panel_order, got, block_rows, "choose_along_x")
    pieces = [piece] + [along_y(piece, s) for s in range(1, cols_count)]
    other = along_rows(load, lambda x, z, c: (x, (z // 2 ^ 1) * 2 + z % 2, c))
    load = jnp.where(masks[0] != 0, other, load)
    other = along_rows(load, lambda x, z, c: (x, (3 - z // 2) * 2 + z % 2, c))
    load = jnp.where(masks[1] != 0, other, load)
    load, *pieces = lax.optimization_barrier((load, *pieces))
    other = along_rows(load, lambda x, z, c: (x, z ^ 1, c))

    def part(array, first):
        at = [(2 * k + first) * part_rows for k in range(PANELS)]
        return [array[lo : lo + part_rows] for lo in at]

    shares = jnp.concatenate(part(load, 0) + part(other, 0), 0)
    rights = jnp.concatenate(part(load, 1) + part(other, 1), 0)
    load = jnp.concatenate([shares] + [along_y(shares, s) for s in range(1, cols_count)] + [rights], 0)
    other = to_core(load)

    v1, rest, under, right = first_call(load, other)
    v2, cross = second_call(rest, under)
    factor, weights, solved, reduced = apply_call(row_block, pieces, v1, cross, v2, right, samples)
    trailing = update_call(kernel, weights, across)
    return trailing, factor, solved, reduced


def solution(mesh):
    in_specs = (P("rows", "cols"), P("rows"), P(), P("rows", "cols"))
    out_specs = (P("rows", "cols"), P("rows", None), P(None, "cols"), P("rows", "cols"))
    return jax.shard_map(
        on_device, mesh=mesh, in_specs=in_specs, out_specs=out_specs, check_vma=False
    )
```

profile of v0, /device:TPU:1, one launch (start us, length us, event | category | flops | bytes accessed | tf_op | source)
XLA Modules:
  0.0 128.2 jit_solution(4090365281799662983)
XLA Ops:
  7.2 0.0 all-gather.2.cloned.1.call-start
  7.2 2.0 %pack_messages.1 = (f32[64,512]{1,0:T(8,128)S(1)}, f32[64,512]{1,0:T(8,128)S(1)}, f32[64,512]{1,0:T(8,128)S(1)}, f32[64,512]{1,0:T(8,128)S(1)}, f32[32,512]{1,0:...) custom-call(s32[2]{0:T(128)} %order_ref.7, ...), custom_call_target="tpu_custom_call" | custom-call | bytes 2000000 | tf_op jit(solution)/shard_map/pack_messages/pallas_call | solution.py:354
  9.3 2.2 %collective-permute-start.8 = (f32[64,512]{1,0:T(8,128)S(1)}, f32[64,512]{1,0:T(8,128)S(1)}, u32[]{:S(2)}, u32[]{:S(2)}) collective-permute-start(f32[64,512]{1,0:T(8,128)S(1)} %get-tuple-element.38), channel_id=1, source_target_pairs={{0,1},{1,2},{2,3},{3,0},{4,5},{5,6},{6,7},{7,4},{8,9},{9,10},{10,1... | collective-permute-start | bytes 393224 | tf_op jit(solution)/shard_map/ppermute | solution.py:443
  11.5 2.6 %collective-permute-start.9 = (f32[64,512]{1,0:T(8,128)S(1)}, f32[64,512]{1,0:T(8,128)S(1)}, u32[]{:S(2)}, u32[]{:S(2)}) collective-permute-start(f32[64,512]{1,0:T(8,128)S(1)} %get-tuple-element.39), channel_id=1, source_target_pairs={{0,2},{1,3},{2,0},{3,1},{4,6},{5,7},{6,4},{7,5},{8,10},{9,11},{10,... | collective-permute-start | bytes 393224 | tf_op jit(solution)/shard_map/ppermute | solution.py:443
  14.1 1.1 collective-permute-start.10
  15.2 0.1 collective-permute-done.8.refs_1_
  15.3 4.5 %collective-permute-done.9.refs_2_ = f32[64,512]{1,0:T(8,128)S(1)} collective-permute-done((f32[64,512]{1,0:T(8,128)S(1)}, f32[64,512]{1,0:T(8,128)S(1)}, u32[]{:S(2)}, u32[]{:S(2)}) %collective-permute-start.9) | collective-permute-done | bytes 131104 | tf_op jit(solution)/shard_map/ppermute | solution.py:443
  19.8 1.3 choose_pieces.1.refs_0_
  21.0 0.0 all-gather.2.cloned.1.call-update
  21.1 0.1 collective-permute-start
  21.2 2.1 %collective-permute-start.1 = (f32[32,512]{1,0:T(8,128)S(1)}, f32[32,512]{1,0:T(8,128)S(1)}, u32[]{:S(2)}, u32[]{:S(2)}) collective-permute-start(f32[32,512]{1,0:T(8,128)S(1)} %get-tuple-element.34), channel_id=1, source_target_pairs={{0,2},{1,3},{2,0},{3,1},{4,6},{5,7},{6,4},{7,5},{8,10},{9,11},{10,... | collective-permute-start | bytes 196616 | tf_op jit(solution)/shard_map/ppermute | solution.py:443
  23.3 1.7 %collective-permute-start.2 = (f32[32,512]{1,0:T(8,128)S(1)}, f32[32,512]{1,0:T(8,128)S(1)}, u32[]{:S(2)}, u32[]{:S(2)}) collective-permute-start(f32[32,512]{1,0:T(8,128)S(1)} %get-tuple-element.35), channel_id=1, source_target_pairs={{0,3},{1,0},{2,1},{3,2},{4,7},{5,4},{6,5},{7,6},{8,11},{9,8},{10,9... | collective-permute-start | bytes 196616 | tf_op jit(solution)/shard_map/ppermute | solution.py:443
  24.9 1.2 collective-permute-done.refs_1_
  26.2 0.0 collective-permute-done.1.refs_2_
  26.2 0.6 collective-permute-done.2.refs_3_
  26.8 0.6 choose_shares.1.refs_0_
  27.4 3.6 %collective-permute-start.5 = (f32[64,512]{1,0:T(8,128)S(1)}, f32[64,512]{1,0:T(8,128)S(1)}, u32[]{:S(2)}, u32[]{:S(2)}) collective-permute-start(f32[64,512]{1,0:T(8,128)S(1)} %choose_shares.1.refs_0_), channel_id=1, source_target_pairs={{0,192},{4,196},{8,200},{12,204},{16,208},{20,212},{24,216},{28,22... | collective-permute-start | bytes 393224 | tf_op jit(solution)/shard_map/ppermute | solution.py:452
  31.0 0.5 collective-permute-start.4
  31.5 0.6 collective-permute-start.3
  32.1 2.2 %collective-permute-done.5.refs_3_ = f32[64,512]{1,0:T(8,128)S(1)} collective-permute-done((f32[64,512]{1,0:T(8,128)S(1)}, f32[64,512]{1,0:T(8,128)S(1)}, u32[]{:S(2)}, u32[]{:S(2)}) %collective-permute-start.5) | collective-permute-done | bytes 131104 | tf_op jit(solution)/shard_map/ppermute | solution.py:452
  34.3 2.1 %collective-permute-done.4.refs_2_ = f32[64,512]{1,0:T(8,128)S(1)} collective-permute-done((f32[64,512]{1,0:T(8,128)S(1)}, f32[64,512]{1,0:T(8,128)S(1)}, u32[]{:S(2)}, u32[]{:S(2)}) %collective-permute-start.4) | collective-permute-done | bytes 131104 | tf_op jit(solution)/shard_map/ppermute | solution.py:452
  36.4 1.3 %collective-permute-done.3.refs_1_ = f32[64,512]{1,0:T(8,128)S(1)} collective-permute-done((f32[64,512]{1,0:T(8,128)S(1)}, f32[64,512]{1,0:T(8,128)S(1)}, u32[]{:S(2)}, u32[]{:S(2)}) %collective-permute-start.3) | collective-permute-done | bytes 131104 | tf_op jit(solution)/shard_map/ppermute | solution.py:452
  37.7 0.6 choose_along_x.1
  38.3 3.1 %collective-permute-start.6 = (f32[64,512]{1,0:T(8,128)S(1)}, f32[64,512]{1,0:T(8,128)S(1)}, u32[]{:S(2)}, u32[]{:S(2)}) collective-permute-start(f32[64,512]{1,0:T(8,128)S(1)} %choose_along_x.1), channel_id=1, source_target_pairs={{0,16},{4,20},{8,24},{12,28},{16,0},{20,4},{24,8},{28,12},{32,48},... | collective-permute-start | bytes 393224 | tf_op jit(solution)/shard_map/ppermute | solution.py:452
  41.4 2.4 %collective-permute-done.6 = f32[64,512]{1,0:T(8,128)S(1)} collective-permute-done((f32[64,512]{1,0:T(8,128)S(1)}, f32[64,512]{1,0:T(8,128)S(1)}, u32[]{:S(2)}, u32[]{:S(2)}) %collective-permute-start.6) | collective-permute-done | bytes 131104 | tf_op jit(solution)/shard_map/ppermute | solution.py:452
  43.8 6.3 %collective-permute-start.7 = (f32[64,512]{1,0:T(8,128)S(1)}, f32[64,512]{1,0:T(8,128)S(1)}, u32[]{:S(2)}, u32[]{:S(2)}) collective-permute-start(f32[64,512]{1,0:T(8,128)S(1)} %compare_select_fusion), channel_id=1, source_target_pairs={{0,48},{4,52},{8,56},{12,60},{16,32},{20,36},{24,40},{28,44},{32,1... | collective-permute-start | bytes 393224 | tf_op jit(solution)/shard_map/ppermute | solution.py:452
  50.1 1.0 collective-permute-start.13
  51.0 0.5 collective-permute-start.12
  51.5 0.7 collective-permute-start.11
  52.2 1.7 %collective-permute-done.7 = f32[64,512]{1,0:T(8,128)S(1)} collective-permute-done((f32[64,512]{1,0:T(8,128)S(1)}, f32[64,512]{1,0:T(8,128)S(1)}, u32[]{:S(2)}, u32[]{:S(2)}) %collective-permute-start.7) | collective-permute-done | bytes 131104 | tf_op jit(solution)/shard_map/ppermute | solution.py:452
  53.9 0.6 collective-permute-done.13.refs_3_
  54.5 2.2 %collective-permute-done.12.refs_2_ = f32[64,512]{1,0:T(8,128)S(1)} collective-permute-done((f32[64,512]{1,0:T(8,128)}, f32[64,512]{1,0:T(8,128)S(1)}, u32[]{:S(2)}, u32[]{:S(2)}) %collective-permute-start.12) | collective-permute-done | bytes 131104 | tf_op jit(solution)/shard_map/ppermute | solution.py:443
  56.7 1.7 %collective-permute-done.11.refs_1_ = f32[64,512]{1,0:T(8,128)S(1)} collective-permute-done((f32[64,512]{1,0:T(8,128)}, f32[64,512]{1,0:T(8,128)S(1)}, u32[]{:S(2)}, u32[]{:S(2)}) %collective-permute-start.11) | collective-permute-done | bytes 131104 | tf_op jit(solution)/shard_map/ppermute | solution.py:443
  58.4 2.4 %collective-permute-start.14 = (f32[64,512]{1,0:T(8,128)S(1)}, f32[64,512]{1,0:T(8,128)S(1)}, u32[]{:S(2)}, u32[]{:S(2)}) collective-permute-start(f32[64,512]{1,0:T(8,128)S(1)} %compare_select_fusion.1), channel_id=1, source_target_pairs={{0,8},{4,12},{8,0},{12,4},{16,24},{20,28},{24,16},{28,20},{32,40},... | collective-permute-start | bytes 393224 | tf_op jit(solution)/shard_map/ppermute | solution.py:452
  60.8 3.1 %collective-permute-done.14 = f32[64,512]{1,0:T(8,128)S(1)} collective-permute-done((f32[64,512]{1,0:T(8,128)S(1)}, f32[64,512]{1,0:T(8,128)S(1)}, u32[]{:S(2)}, u32[]{:S(2)}) %collective-permute-start.14) | collective-permute-done | bytes 131104 | tf_op jit(solution)/shard_map/ppermute | solution.py:452
  64.0 1.4 %collective-permute-start.17 = (f32[64,512]{1,0:T(8,128)S(1)}, f32[64,512]{1,0:T(8,128)S(1)}, u32[]{:S(2)}, u32[]{:S(2)}) collective-permute-start(f32[64,512]{1,0:T(8,128)S(1)} %pad_maximum_fusion), channel_id=1, source_target_pairs={{0,3},{1,0},{2,1},{3,2},{4,7},{5,4},{6,5},{7,6},{8,11},{9,8},{10,9... | collective-permute-start | bytes 393224 | tf_op jit(solution)/shard_map/ppermute | solution.py:443
  65.4 0.9 collective-permute-start.16
  66.3 0.0 collective-permute-start.15
  66.3 5.8 %collective-permute-done.15 = f32[64,512]{1,0:T(8,128)S(1)} collective-permute-done((f32[64,512]{1,0:T(8,128)S(1)}, f32[64,512]{1,0:T(8,128)S(1)}, u32[]{:S(2)}, u32[]{:S(2)}) %collective-permute-start.15) | collective-permute-done | bytes 131104 | tf_op jit(solution)/shard_map/ppermute | solution.py:443
  72.3 10.2 %collective-permute-start.18 = (f32[320,512]{1,0:T(8,128)S(1)}, f32[320,512]{1,0:T(8,128)S(1)}, u32[]{:S(2)}, u32[]{:S(2)}) collective-permute-start(f32[320,512]{1,0:T(8,128)S(1)} %slice_dynamic-update-slice_fusion.own_ref), channel_id=1, source_target_pairs={{0,4},{4,0},{8,12},{12,8},{16,20},{20,16},{24,28},{28,24},{32,36},... | collective-permute-start | bytes 1966088 | tf_op jit(solution)/shard_map/ppermute | solution.py:452
  82.4 1.7 %collective-permute-done.18.other_ref = f32[320,512]{1,0:T(8,128)S(1)} collective-permute-done((f32[320,512]{1,0:T(8,128)S(1)}, f32[320,512]{1,0:T(8,128)S(1)}, u32[]{:S(2)}, u32[]{:S(2)}) %collective-permute-start.18) | collective-permute-done | bytes 655392 | tf_op jit(solution)/shard_map/ppermute | solution.py:452
  84.2 11.4 %eliminate_first.1 = (f32[256,256]{1,0:T(8,128)S(1)}, f32[256,256]{1,0:T(8,128)S(1)}, f32[256,256]{1,0:T(8,128)S(1)}, f32[512,128]{1,0:T(8,128)S(1)}) custom-call(f32[320,512]{1,0:T(8,128)S(1)} %slice_dynamic-update-slice_fusion.own_ref, f32[320,512]{1,0:T(8,128)S(1)} %collective-permute-done.18.other_ref), custom_call_target="tpu_custom_call" | custom-call | flops 12000000000 | bytes 2000000 | tf_op jit(solution)/shard_map/eliminate_first/pallas_call | solution.py:158
  95.6 0.0 copy-start.1
  95.6 0.0 copy-start.3
  95.7 10.8 %eliminate_second.1 = (f32[256,256]{1,0:T(8,128)S(1)}, f32[256,256]{1,0:T(8,128)S(1)}) custom-call(f32[256,256]{1,0:T(8,128)S(1)} %get-tuple-element.47.rest_ref, f32[256,256]{1,0:T(8,128)S(1)} %get-tuple-element.48.under_ref), custom_call_target="tpu_custom_call" | custom-call | flops 12000000000 | bytes 2000000 | tf_op jit(solution)/shard_map/eliminate_second/pallas_call | solution.py:180
  106.5 5.4 %apply_factor.1 = (f32[256,512]{1,0:T(8,128)}, f32[256,512]{1,0:T(8,128)S(1)}, f32[512,128]{1,0:T(8,128)}, f32[256,128]{1,0:T(8,128)}) custom-call(s32[4]{0:T(128)S(1)} %copy-done.3, f32[64,512]{1,0:T(8,128)} %choose_pieces.1.refs_0_, f32[64,512]{1,0:T(8,128)S(1)} %collective-permute-done.11.refs_1_, f32[64,512]{1,0:T(8,128)S(1)} %collective-permute-done.12.refs_2_, ...), custom_call_target="tpu_custom_call" | custom-call | flops 4000000000 | bytes 4000000 | tf_op jit(solution)/shard_map/apply_factor/pallas_call | solution.py:227
  111.9 0.9 copy-done
  112.8 8.6 %trailing_update.1 = f32[256,4096]{1,0:T(8,128)} custom-call(f32[256,4096]{1,0:T(8,128)} %k_ref.1, f32[256,512]{1,0:T(8,128)} %copy-done, f32[4096,512]{1,0:T(8,128)} %all-gather.2.cloned.1.call-done.b_ref), custom_call_target="tpu_custom_call" | custom-call | flops 3221225472 | bytes 16000000 | tf_op jit(solution)/shard_map/trailing_update/pallas_call | solution.py:274
  (23 shorter events, 0.2 us)
Async XLA Ops:
  7.2 12.6 %copy-start.2 = (s32[2]{0:T(128)S(1)}, s32[2]{0:T(128)}, u32[]{:S(2)}) copy-start(s32[2]{0:T(128)} %order_ref.7) | copy-start | bytes 28
  7.2 105.6 %all-gather.2.cloned.1.call-start = ((), (), s32[]{:S(2)}) async-start(), calls=%async_computation | async-start | bytes 8519680 | tf_op jit(solution)/shard_map/all_gather | solution.py:463
  9.3 6.0 %collective-permute-start.8 = (f32[64,512]{1,0:T(8,128)S(1)}, f32[64,512]{1,0:T(8,128)S(1)}, u32[]{:S(2)}, u32[]{:S(2)}) collective-permute-start(f32[64,512]{1,0:T(8,128)S(1)} %get-tuple-element.38), channel_id=1, source_target_pairs={{0,1},{1,2},{2,3},{3,0},{4,5},{5,6},{6,7},{7,4},{8,9},{9,10},{10,1... | collective-permute-start | bytes 393224 | tf_op jit(solution)/shard_map/ppermute | solution.py:443
  11.5 8.3 %collective-permute-start.9 = (f32[64,512]{1,0:T(8,128)S(1)}, f32[64,512]{1,0:T(8,128)S(1)}, u32[]{:S(2)}, u32[]{:S(2)}) collective-permute-start(f32[64,512]{1,0:T(8,128)S(1)} %get-tuple-element.39), channel_id=1, source_target_pairs={{0,2},{1,3},{2,0},{3,1},{4,6},{5,7},{6,4},{7,5},{8,10},{9,11},{10,... | collective-permute-start | bytes 393224 | tf_op jit(solution)/shard_map/ppermute | solution.py:443
  14.1 5.7 %collective-permute-start.10 = (f32[64,512]{1,0:T(8,128)S(1)}, f32[64,512]{1,0:T(8,128)S(1)}, u32[]{:S(2)}, u32[]{:S(2)}) collective-permute-start(f32[64,512]{1,0:T(8,128)S(1)} %get-tuple-element.40), channel_id=1, source_target_pairs={{0,3},{1,0},{2,1},{3,2},{4,7},{5,4},{6,5},{7,6},{8,11},{9,8},{10,9... | collective-permute-start | bytes 393224 | tf_op jit(solution)/shard_map/ppermute | solution.py:443
  21.1 5.1 %collective-permute-start = (f32[32,512]{1,0:T(8,128)S(1)}, f32[32,512]{1,0:T(8,128)S(1)}, u32[]{:S(2)}, u32[]{:S(2)}) collective-permute-start(f32[32,512]{1,0:T(8,128)S(1)} %get-tuple-element.33), channel_id=1, source_target_pairs={{0,1},{1,2},{2,3},{3,0},{4,5},{5,6},{6,7},{7,4},{8,9},{9,10},{10,1... | collective-permute-start | bytes 196616 | tf_op jit(solution)/shard_map/ppermute | solution.py:443
  21.2 5.0 %collective-permute-start.1 = (f32[32,512]{1,0:T(8,128)S(1)}, f32[32,512]{1,0:T(8,128)S(1)}, u32[]{:S(2)}, u32[]{:S(2)}) collective-permute-start(f32[32,512]{1,0:T(8,128)S(1)} %get-tuple-element.34), channel_id=1, source_target_pairs={{0,2},{1,3},{2,0},{3,1},{4,6},{5,7},{6,4},{7,5},{8,10},{9,11},{10,... | collective-permute-start | bytes 196616 | tf_op jit(solution)/shard_map/ppermute | solution.py:443
  23.3 3.5 %collective-permute-start.2 = (f32[32,512]{1,0:T(8,128)S(1)}, f32[32,512]{1,0:T(8,128)S(1)}, u32[]{:S(2)}, u32[]{:S(2)}) collective-permute-start(f32[32,512]{1,0:T(8,128)S(1)} %get-tuple-element.35), channel_id=1, source_target_pairs={{0,3},{1,0},{2,1},{3,2},{4,7},{5,4},{6,5},{7,6},{8,11},{9,8},{10,9... | collective-permute-start | bytes 196616 | tf_op jit(solution)/shard_map/ppermute | solution.py:443
  27.4 7.0 %collective-permute-start.5 = (f32[64,512]{1,0:T(8,128)S(1)}, f32[64,512]{1,0:T(8,128)S(1)}, u32[]{:S(2)}, u32[]{:S(2)}) collective-permute-start(f32[64,512]{1,0:T(8,128)S(1)} %choose_shares.1.refs_0_), channel_id=1, source_target_pairs={{0,192},{4,196},{8,200},{12,204},{16,208},{20,212},{24,216},{28,22... | collective-permute-start | bytes 393224 | tf_op jit(solution)/shard_map/ppermute | solution.py:452
  31.0 5.4 %collective-permute-start.4 = (f32[64,512]{1,0:T(8,128)S(1)}, f32[64,512]{1,0:T(8,128)S(1)}, u32[]{:S(2)}, u32[]{:S(2)}) collective-permute-start(f32[64,512]{1,0:T(8,128)S(1)} %choose_shares.1.refs_0_), channel_id=1, source_target_pairs={{0,128},{4,132},{8,136},{12,140},{16,144},{20,148},{24,152},{28,15... | collective-permute-start | bytes 393224 | tf_op jit(solution)/shard_map/ppermute | solution.py:452
  31.5 6.2 %collective-permute-start.3 = (f32[64,512]{1,0:T(8,128)S(1)}, f32[64,512]{1,0:T(8,128)S(1)}, u32[]{:S(2)}, u32[]{:S(2)}) collective-permute-start(f32[64,512]{1,0:T(8,128)S(1)} %choose_shares.1.refs_0_), channel_id=1, source_target_pairs={{0,64},{4,68},{8,72},{12,76},{16,80},{20,84},{24,88},{28,92},{32,9... | collective-permute-start | bytes 393224 | tf_op jit(solution)/shard_map/ppermute | solution.py:452
  38.3 5.4 %collective-permute-start.6 = (f32[64,512]{1,0:T(8,128)S(1)}, f32[64,512]{1,0:T(8,128)S(1)}, u32[]{:S(2)}, u32[]{:S(2)}) collective-permute-start(f32[64,512]{1,0:T(8,128)S(1)} %choose_along_x.1), channel_id=1, source_target_pairs={{0,16},{4,20},{8,24},{12,28},{16,0},{20,4},{24,8},{28,12},{32,48},... | collective-permute-start | bytes 393224 | tf_op jit(solution)/shard_map/ppermute | solution.py:452
  43.8 10.1 %collective-permute-start.7 = (f32[64,512]{1,0:T(8,128)S(1)}, f32[64,512]{1,0:T(8,128)S(1)}, u32[]{:S(2)}, u32[]{:S(2)}) collective-permute-start(f32[64,512]{1,0:T(8,128)S(1)} %compare_select_fusion), channel_id=1, source_target_pairs={{0,48},{4,52},{8,56},{12,60},{16,32},{20,36},{24,40},{28,44},{32,1... | collective-permute-start | bytes 393224 | tf_op jit(solution)/shard_map/ppermute | solution.py:452
  50.1 4.4 %collective-permute-start.13 = (f32[64,512]{1,0:T(8,128)}, f32[64,512]{1,0:T(8,128)S(1)}, u32[]{:S(2)}, u32[]{:S(2)}) collective-permute-start(f32[64,512]{1,0:T(8,128)} %choose_pieces.1.refs_0_), channel_id=1, source_target_pairs={{0,3},{1,0},{2,1},{3,2},{4,7},{5,4},{6,5},{7,6},{8,11},{9,8},{10,9... | collective-permute-start | bytes 393224 | tf_op jit(solution)/shard_map/ppermute | solution.py:443
  51.0 5.6 %collective-permute-start.12 = (f32[64,512]{1,0:T(8,128)}, f32[64,512]{1,0:T(8,128)S(1)}, u32[]{:S(2)}, u32[]{:S(2)}) collective-permute-start(f32[64,512]{1,0:T(8,128)} %choose_pieces.1.refs_0_), channel_id=1, source_target_pairs={{0,2},{1,3},{2,0},{3,1},{4,6},{5,7},{6,4},{7,5},{8,10},{9,11},{10,... | collective-permute-start | bytes 393224 | tf_op jit(solution)/shard_map/ppermute | solution.py:443
  51.5 6.8 %collective-permute-start.11 = (f32[64,512]{1,0:T(8,128)}, f32[64,512]{1,0:T(8,128)S(1)}, u32[]{:S(2)}, u32[]{:S(2)}) collective-permute-start(f32[64,512]{1,0:T(8,128)} %choose_pieces.1.refs_0_), channel_id=1, source_target_pairs={{0,1},{1,2},{2,3},{3,0},{4,5},{5,6},{6,7},{7,4},{8,9},{9,10},{10,1... | collective-permute-start | bytes 393224 | tf_op jit(solution)/shard_map/ppermute | solution.py:443
  58.4 5.6 %collective-permute-start.14 = (f32[64,512]{1,0:T(8,128)S(1)}, f32[64,512]{1,0:T(8,128)S(1)}, u32[]{:S(2)}, u32[]{:S(2)}) collective-permute-start(f32[64,512]{1,0:T(8,128)S(1)} %compare_select_fusion.1), channel_id=1, source_target_pairs={{0,8},{4,12},{8,0},{12,4},{16,24},{20,28},{24,16},{28,20},{32,40},... | collective-permute-start | bytes 393224 | tf_op jit(solution)/shard_map/ppermute | solution.py:452
  64.0 8.2 %collective-permute-start.17 = (f32[64,512]{1,0:T(8,128)S(1)}, f32[64,512]{1,0:T(8,128)S(1)}, u32[]{:S(2)}, u32[]{:S(2)}) collective-permute-start(f32[64,512]{1,0:T(8,128)S(1)} %pad_maximum_fusion), channel_id=1, source_target_pairs={{0,3},{1,0},{2,1},{3,2},{4,7},{5,4},{6,5},{7,6},{8,11},{9,8},{10,9... | collective-permute-start | bytes 393224 | tf_op jit(solution)/shard_map/ppermute | solution.py:443
  65.4 6.7 %collective-permute-start.16 = (f32[64,512]{1,0:T(8,128)S(1)}, f32[64,512]{1,0:T(8,128)S(1)}, u32[]{:S(2)}, u32[]{:S(2)}) collective-permute-start(f32[64,512]{1,0:T(8,128)S(1)} %pad_maximum_fusion), channel_id=1, source_target_pairs={{0,2},{1,3},{2,0},{3,1},{4,6},{5,7},{6,4},{7,5},{8,10},{9,11},{10,... | collective-permute-start | bytes 393224 | tf_op jit(solution)/shard_map/ppermute | solution.py:443
  66.3 5.8 %collective-permute-start.15 = (f32[64,512]{1,0:T(8,128)S(1)}, f32[64,512]{1,0:T(8,128)S(1)}, u32[]{:S(2)}, u32[]{:S(2)}) collective-permute-start(f32[64,512]{1,0:T(8,128)S(1)} %pad_maximum_fusion), channel_id=1, source_target_pairs={{0,1},{1,2},{2,3},{3,0},{4,5},{5,6},{6,7},{7,4},{8,9},{9,10},{10,1... | collective-permute-start | bytes 393224 | tf_op jit(solution)/shard_map/ppermute | solution.py:443
  72.3 11.9 %collective-permute-start.18 = (f32[320,512]{1,0:T(8,128)S(1)}, f32[320,512]{1,0:T(8,128)S(1)}, u32[]{:S(2)}, u32[]{:S(2)}) collective-permute-start(f32[320,512]{1,0:T(8,128)S(1)} %slice_dynamic-update-slice_fusion.own_ref), channel_id=1, source_target_pairs={{0,4},{4,0},{8,12},{12,8},{16,20},{20,16},{24,28},{28,24},{32,36},... | collective-permute-start | bytes 1966088 | tf_op jit(solution)/shard_map/ppermute | solution.py:452
  95.6 10.8 %copy-start.1 = (f32[256,128]{1,0:T(8,128)S(1)}, f32[256,128]{1,0:T(8,128)}, u32[]{:S(2)}) copy-start(f32[256,128]{1,0:T(8,128)} %refs_8_.1) | copy-start | bytes 393220
  95.6 10.8 %copy-start.3 = (s32[4]{0:T(128)S(1)}, s32[4]{0:T(128)}, u32[]{:S(2)}) copy-start(s32[4]{0:T(128)} %block_ref.3) | copy-start | bytes 52
  111.9 0.9 copy-start
Sparse Core Ops, SparseCore 0:
  21.2 86.8 all-gather.1
where the time goes:
time: 128 us
  starting transfers between devices  41 us (32%)
  Pallas kernels  40.7 us (32%)
  waiting for transfers between devices  31.2 us (24%)
  between operations  14.2 us (11%)
    ppermute x7, starting transfers between devices, along_rows(): return lax.ppermute(array, 'rows', pairs)  26.7 us
    ppermute x12, waiting for transfers between devices, along_y(): lax.ppermute(array, 'cols', [(i, (i + shift) % cols_count) for i in range...  16.7 us
    ppermute x7, waiting for transfers between devices, along_rows(): return lax.ppermute(array, 'rows', pairs)  14.5 us
    ppermute x12, starting transfers between devices, along_y(): lax.ppermute(array, 'cols', [(i, (i + shift) % cols_count) for i in range...  14.2 us
    pallas_call x1, Pallas kernels, first_call(): pl.pallas_call(first_kernel, out_shape=[square(PW), square(PW), square(PW...  11.4 us
    pallas_call x1, Pallas kernels, second_call(): pl.pallas_call(second_kernel, out_shape=[square(PW), square(PW)], scratch...  10.8 us
    pallas_call x1, Pallas kernels, update_call(): pl.pallas_call(update_kernel, in_specs=[pl.BlockSpec(memory_space=pltpu.H...  8.59 us
    pallas_call x1, Pallas kernels, apply_call(): pl.pallas_call(apply_kernel, in_specs=[pl.BlockSpec(memory_space=pltpu.SM...  5.41 us
  transfers between devices with their start and end apart: 20, of which 15 were waited for; matrix products, arithmetic and copies ran while one was open for 0% of the time, Pallas kernels for 23%

commit v1 on v0

--- a/solution.py
+++ b/solution.py
@@ -241,7 +241,7 @@
     )(row_block, *operands)
 
 
-WIDTH = 512
+WIDTH = 1024
 
 
 def update_kernel(k_ref, w_ref, b_ref, o_ref, held, gathered, out, k_sems, b_sems, out_sems):
@@ -252,12 +252,15 @@
     for b_load, k_load in zip(b_loads, k_loads):
         b_load.start()
         k_load.start()
+    rows = w_ref.shape[0]
     wh, wl = halves(w_ref[...])
+    both = jnp.concatenate([wh, wl], 0)
     stores = []
     for i, at in enumerate(parts):
         b_loads[i].wait()
         top, bottom = halves(gathered[at])
-        total = dot_nt(wh, top, None) + dot_nt(wh, bottom, None) + dot_nt(wl, top, None)
+        wide = dot_nt(both, top, None)
+        total = wide[:rows] + wide[rows:] + dot_nt(wh, bottom, None)
         k_loads[i].wait()
         out[:, at] = held[:, at] - total
         stores.append(pltpu.make_async_copy(out.at[:, at], o_ref.at[:, at], out_sems.at[i]))
@@ -466,12 +469,10 @@
 
     got = [load] + [along_x(load, s) for s in range(1, 4)]
     load = choose_call(load_kernel, panel_order, got, block_rows, "choose_along_x")
-    pieces = [piece] + [along_y(piece, s) for s in range(1, cols_count)]
     other = along_rows(load, lambda x, z, c: (x, (z // 2 ^ 1) * 2 + z % 2, c))
     load = jnp.where(masks[0] != 0, other, load)
     other = along_rows(load, lambda x, z, c: (x, (3 - z // 2) * 2 + z % 2, c))
     load = jnp.where(masks[1] != 0, other, load)
-    load, *pieces = lax.optimization_barrier((load, *pieces))
     other = along_rows(load, lambda x, z, c: (x, z ^ 1, c))
 
     def part(array, first):
@@ -482,8 +483,11 @@
     rights = jnp.concatenate(part(load, 1) + part(other, 1), 0)
     load = jnp.concatenate([shares] + [along_y(shares, s) for s in range(1, cols_count)] + [rights], 0)
     other = to_core(load)
+    load, piece = lax.optimization_barrier((load, piece))
+    pieces = [piece] + [along_y(piece, s) for s in range(1, cols_count)]
 
     v1, rest, under, right = first_call(load, other)
+    rest, under, *pieces = lax.optimization_barrier((rest, under, *pieces))
     v2, cross = second_call(rest, under)
     factor, weights, solved, reduced = apply_call(row_block, pieces, v1, cross, v2, right, samples)
     trailing = update_call(kernel, weights, across)

time: 128 us -> 124 us (0.969)
  waiting for transfers between devices: 31.2 us -> 26.8 us
    ppermute x12, waiting for transfers between devices: 16.7 us -> 11.7 us  [along_y(): lax.ppermute(array, 'cols', [(i, (i + shift) % cols_count) for i in range...]
    ppermute x7, starting transfers between devices: 26.7 us -> 28 us  [along_rows(): return lax.ppermute(array, 'rows', pairs)]
  transfers between devices with their start and end apart: 20 -> 20, of which waited for: 15 -> 12; matrix products, arithmetic and copies ran while one was open for 0% -> 0% of each run, Pallas kernels for 23% -> 23%
where the time goes in v1:
time: 124 us
  starting transfers between devices  41.7 us (34%)
  Pallas kernels  40.3 us (32%)
  waiting for transfers between devices  26.8 us (22%)
  between operations  14.3 us (12%)
    ppermute x7, starting transfers between devices, along_rows(): return lax.ppermute(array, 'rows', pairs)  28 us
    ppermute x7, waiting for transfers between devices, along_rows(): return lax.ppermute(array, 'rows', pairs)  15.2 us
    ppermute x12, starting transfers between devices, along_y(): lax.ppermute(array, 'cols', [(i, (i + shift) % cols_count) for i in range...  13.6 us
    ppermute x12, waiting for transfers between devices, along_y(): lax.ppermute(array, 'cols', [(i, (i + shift) % cols_count) for i in range...  11.7 us
    pallas_call x1, Pallas kernels, first_call(): pl.pallas_call(first_kernel, out_shape=[square(PW), square(PW), square(PW...  11.4 us
    pallas_call x1, Pallas kernels, second_call(): pl.pallas_call(second_kernel, out_shape=[square(PW), square(PW)], scratch...  10.8 us
    pallas_call x1, Pallas kernels, update_call(): pl.pallas_call(update_kernel, in_specs=[pl.BlockSpec(memory_space=pltpu.H...  8.16 us
    pallas_call x1, Pallas kernels, apply_call(): pl.pallas_call(apply_kernel, in_specs=[pl.BlockSpec(memory_space=pltpu.SM...  5.45 us
  transfers between devices with their start and end apart: 20, of which 12 were waited for; matrix products, arithmetic and copies ran while one was open for 0% of the time, Pallas kernels for 23%

profile of v1, /device:TPU:1, one launch (start us, length us, event | category | flops | bytes accessed | tf_op | source)
XLA Modules:
  0.0 124.2 jit_solution(17532601386926519587)
XLA Ops:
  7.2 0.0 all-gather.2.cloned.1.call-start
  7.2 2.0 %pack_messages.1 = (f32[64,512]{1,0:T(8,128)S(1)}, f32[64,512]{1,0:T(8,128)S(1)}, f32[64,512]{1,0:T(8,128)S(1)}, f32[64,512]{1,0:T(8,128)S(1)}, f32[32,512]{1,0:...) custom-call(s32[2]{0:T(128)} %order_ref.7, ...), custom_call_target="tpu_custom_call" | custom-call | bytes 2000000 | tf_op jit(solution)/shard_map/pack_messages/pallas_call | solution.py:357
  9.3 2.2 %collective-permute-start.12 = (f32[64,512]{1,0:T(8,128)S(1)}, f32[64,512]{1,0:T(8,128)S(1)}, u32[]{:S(2)}, u32[]{:S(2)}) collective-permute-start(f32[64,512]{1,0:T(8,128)S(1)} %get-tuple-element.41), channel_id=1, source_target_pairs={{0,1},{1,2},{2,3},{3,0},{4,5},{5,6},{6,7},{7,4},{8,9},{9,10},{10,1... | collective-permute-start | bytes 393224 | tf_op jit(solution)/shard_map/ppermute | solution.py:446
  11.5 2.6 %collective-permute-start.13 = (f32[64,512]{1,0:T(8,128)S(1)}, f32[64,512]{1,0:T(8,128)S(1)}, u32[]{:S(2)}, u32[]{:S(2)}) collective-permute-start(f32[64,512]{1,0:T(8,128)S(1)} %get-tuple-element.42), channel_id=1, source_target_pairs={{0,2},{1,3},{2,0},{3,1},{4,6},{5,7},{6,4},{7,5},{8,10},{9,11},{10,... | collective-permute-start | bytes 393224 | tf_op jit(solution)/shard_map/ppermute | solution.py:446
  14.1 1.1 collective-permute-start.14
  15.2 0.1 collective-permute-done.12.refs_1_
  15.3 4.5 %collective-permute-done.13.refs_2_ = f32[64,512]{1,0:T(8,128)S(1)} collective-permute-done((f32[64,512]{1,0:T(8,128)S(1)}, f32[64,512]{1,0:T(8,128)S(1)}, u32[]{:S(2)}, u32[]{:S(2)}) %collective-permute-start.13) | collective-permute-done | bytes 131104 | tf_op jit(solution)/shard_map/ppermute | solution.py:446
  19.8 1.3 %choose_pieces.1.refs_0_ = f32[64,512]{1,0:T(8,128)} custom-call(s32[2]{0:T(128)S(1)} %copy-done.2, f32[64,512]{1,0:T(8,128)S(1)} %get-tuple-element.40.refs_0_, f32[64,512]{1,0:T(8,128)S(1)} %collective-permute-done.12.refs_1_, f32[64,512]{1,0:T(8,128)S(1)} %collective-permute-done.13.refs_2_, f32[64,512]{1,0:T(8,128)S(1)} %collective-permute-done.14.refs_3_), custom_call_target="tpu_custom_call" | custom-call | bytes 1000000 | tf_op jit(solution)/shard_map/choose_pieces/pallas_call | solution.py:430
  21.0 0.0 all-gather.2.cloned.1.call-update
  21.1 0.1 collective-permute-start
  21.2 2.1 %collective-permute-start.1 = (f32[32,512]{1,0:T(8,128)S(1)}, f32[32,512]{1,0:T(8,128)S(1)}, u32[]{:S(2)}, u32[]{:S(2)}) collective-permute-start(f32[32,512]{1,0:T(8,128)S(1)} %get-tuple-element.37), channel_id=1, source_target_pairs={{0,2},{1,3},{2,0},{3,1},{4,6},{5,7},{6,4},{7,5},{8,10},{9,11},{10,... | collective-permute-start | bytes 196616 | tf_op jit(solution)/shard_map/ppermute | solution.py:446
  23.3 1.7 %collective-permute-start.2 = (f32[32,512]{1,0:T(8,128)S(1)}, f32[32,512]{1,0:T(8,128)S(1)}, u32[]{:S(2)}, u32[]{:S(2)}) collective-permute-start(f32[32,512]{1,0:T(8,128)S(1)} %get-tuple-element.38), channel_id=1, source_target_pairs={{0,3},{1,0},{2,1},{3,2},{4,7},{5,4},{6,5},{7,6},{8,11},{9,8},{10,9... | collective-permute-start | bytes 196616 | tf_op jit(solution)/shard_map/ppermute | solution.py:446
  24.9 1.2 collective-permute-done.refs_1_
  26.2 0.0 collective-permute-done.1.refs_2_
  26.2 0.6 collective-permute-done.2.refs_3_
  26.8 0.6 choose_shares.1.refs_0_
  27.4 3.6 %collective-permute-start.5 = (f32[64,512]{1,0:T(8,128)S(1)}, f32[64,512]{1,0:T(8,128)S(1)}, u32[]{:S(2)}, u32[]{:S(2)}) collective-permute-start(f32[64,512]{1,0:T(8,128)S(1)} %choose_shares.1.refs_0_), channel_id=1, source_target_pairs={{0,192},{4,196},{8,200},{12,204},{16,208},{20,212},{24,216},{28,22... | collective-permute-start | bytes 393224 | tf_op jit(solution)/shard_map/ppermute | solution.py:455
  31.0 0.5 collective-permute-start.4
  31.5 0.6 collective-permute-start.3
  32.1 2.2 %collective-permute-done.5.refs_3_ = f32[64,512]{1,0:T(8,128)S(1)} collective-permute-done((f32[64,512]{1,0:T(8,128)S(1)}, f32[64,512]{1,0:T(8,128)S(1)}, u32[]{:S(2)}, u32[]{:S(2)}) %collective-permute-start.5) | collective-permute-done | bytes 131104 | tf_op jit(solution)/shard_map/ppermute | solution.py:455
  34.3 2.1 %collective-permute-done.4.refs_2_ = f32[64,512]{1,0:T(8,128)S(1)} collective-permute-done((f32[64,512]{1,0:T(8,128)S(1)}, f32[64,512]{1,0:T(8,128)S(1)}, u32[]{:S(2)}, u32[]{:S(2)}) %collective-permute-start.4) | collective-permute-done | bytes 131104 | tf_op jit(solution)/shard_map/ppermute | solution.py:455
  36.4 1.3 %collective-permute-done.3.refs_1_ = f32[64,512]{1,0:T(8,128)S(1)} collective-permute-done((f32[64,512]{1,0:T(8,128)S(1)}, f32[64,512]{1,0:T(8,128)S(1)}, u32[]{:S(2)}, u32[]{:S(2)}) %collective-permute-start.3) | collective-permute-done | bytes 131104 | tf_op jit(solution)/shard_map/ppermute | solution.py:455
  37.7 0.6 choose_along_x.1
  38.3 3.1 %collective-permute-start.6 = (f32[64,512]{1,0:T(8,128)S(1)}, f32[64,512]{1,0:T(8,128)S(1)}, u32[]{:S(2)}, u32[]{:S(2)}) collective-permute-start(f32[64,512]{1,0:T(8,128)S(1)} %choose_along_x.1), channel_id=1, source_target_pairs={{0,16},{4,20},{8,24},{12,28},{16,0},{20,4},{24,8},{28,12},{32,48},... | collective-permute-start | bytes 393224 | tf_op jit(solution)/shard_map/ppermute | solution.py:455
  41.4 2.4 %collective-permute-done.6 = f32[64,512]{1,0:T(8,128)S(1)} collective-permute-done((f32[64,512]{1,0:T(8,128)S(1)}, f32[64,512]{1,0:T(8,128)S(1)}, u32[]{:S(2)}, u32[]{:S(2)}) %collective-permute-start.6) | collective-permute-done | bytes 131104 | tf_op jit(solution)/shard_map/ppermute | solution.py:455
  43.8 6.3 %collective-permute-start.7 = (f32[64,512]{1,0:T(8,128)S(1)}, f32[64,512]{1,0:T(8,128)S(1)}, u32[]{:S(2)}, u32[]{:S(2)}) collective-permute-start(f32[64,512]{1,0:T(8,128)S(1)} %compare_select_fusion), channel_id=1, source_target_pairs={{0,48},{4,52},{8,56},{12,60},{16,32},{20,36},{24,40},{28,44},{32,1... | collective-permute-start | bytes 393224 | tf_op jit(solution)/shard_map/ppermute | solution.py:455
  50.1 3.8 %collective-permute-done.7 = f32[64,512]{1,0:T(8,128)S(1)} collective-permute-done((f32[64,512]{1,0:T(8,128)S(1)}, f32[64,512]{1,0:T(8,128)S(1)}, u32[]{:S(2)}, u32[]{:S(2)}) %collective-permute-start.7) | collective-permute-done | bytes 131104 | tf_op jit(solution)/shard_map/ppermute | solution.py:455
  53.9 2.2 %collective-permute-start.8 = (f32[64,512]{1,0:T(8,128)S(1)}, f32[64,512]{1,0:T(8,128)S(1)}, u32[]{:S(2)}, u32[]{:S(2)}) collective-permute-start(f32[64,512]{1,0:T(8,128)S(1)} %compare_select_fusion.1), channel_id=1, source_target_pairs={{0,8},{4,12},{8,0},{12,4},{16,24},{20,28},{24,16},{28,20},{32,40},... | collective-permute-start | bytes 393224 | tf_op jit(solution)/shard_map/ppermute | solution.py:455
  56.2 3.1 %collective-permute-done.8 = f32[64,512]{1,0:T(8,128)S(1)} collective-permute-done((f32[64,512]{1,0:T(8,128)S(1)}, f32[64,512]{1,0:T(8,128)S(1)}, u32[]{:S(2)}, u32[]{:S(2)}) %collective-permute-start.8) | collective-permute-done | bytes 131104 | tf_op jit(solution)/shard_map/ppermute | solution.py:455
  59.4 0.9 collective-permute-start.11
  60.2 0.8 collective-permute-start.10
  61.0 0.7 collective-permute-start.9
  61.8 5.2 %collective-permute-done.9 = f32[64,512]{1,0:T(8,128)S(1)} collective-permute-done((f32[64,512]{1,0:T(8,128)S(1)}, f32[64,512]{1,0:T(8,128)S(1)}, u32[]{:S(2)}, u32[]{:S(2)}) %collective-permute-start.9) | collective-permute-done | bytes 131104 | tf_op jit(solution)/shard_map/ppermute | solution.py:446
  67.0 0.0 collective-permute-done.10
  67.0 0.0 collective-permute-done.11
  67.1 11.7 %collective-permute-start.15 = (f32[320,512]{1,0:T(8,128)S(1)}, f32[320,512]{1,0:T(8,128)S(1)}, u32[]{:S(2)}, u32[]{:S(2)}) collective-permute-start(f32[320,512]{1,0:T(8,128)S(1)} %slice_dynamic-update-slice_fusion.own_ref), channel_id=1, source_target_pairs={{0,4},{4,0},{8,12},{12,8},{16,20},{20,16},{24,28},{28,24},{32,36},... | collective-permute-start | bytes 1966088 | tf_op jit(solution)/shard_map/ppermute | solution.py:455
  78.8 0.3 collective-permute-start.18
  79.1 0.1 collective-permute-start.17
  79.1 1.1 collective-permute-start.16
  80.2 0.2 collective-permute-done.15.other_ref
  80.5 11.4 %eliminate_first.1 = (f32[256,256]{1,0:T(8,128)S(1)}, f32[256,256]{1,0:T(8,128)S(1)}, f32[256,256]{1,0:T(8,128)S(1)}, f32[512,128]{1,0:T(8,128)S(1)}) custom-call(f32[320,512]{1,0:T(8,128)S(1)} %slice_dynamic-update-slice_fusion.own_ref, f32[320,512]{1,0:T(8,128)S(1)} %collective-permute-done.15.other_ref), custom_call_target="tpu_custom_call" | custom-call | flops 12000000000 | bytes 2000000 | tf_op jit(solution)/shard_map/eliminate_first/pallas_call | solution.py:158
  91.9 0.0 collective-permute-done.18.refs_3_
  92.0 0.0 copy-start.1
  92.0 0.0 copy-start.3
  92.0 10.8 %eliminate_second.1 = (f32[256,256]{1,0:T(8,128)S(1)}, f32[256,256]{1,0:T(8,128)S(1)}) custom-call(f32[256,256]{1,0:T(8,128)S(1)} %get-tuple-element.53.rest_ref, f32[256,256]{1,0:T(8,128)S(1)} %get-tuple-element.54.under_ref), custom_call_target="tpu_custom_call" | custom-call | flops 12000000000 | bytes 2000000 | tf_op jit(solution)/shard_map/eliminate_second/pallas_call | solution.py:180
  102.8 5.5 %apply_factor.1 = (f32[256,512]{1,0:T(8,128)}, f32[256,512]{1,0:T(8,128)S(1)}, f32[512,128]{1,0:T(8,128)}, f32[256,128]{1,0:T(8,128)}) custom-call(s32[4]{0:T(128)S(1)} %copy-done.3, f32[64,512]{1,0:T(8,128)} %choose_pieces.1.refs_0_, f32[64,512]{1,0:T(8,128)S(1)} %collective-permute-done.16.refs_1_, f32[64,512]{1,0:T(8,128)S(1)} %collective-permute-done.17.refs_2_, ...), custom_call_target="tpu_custom_call" | custom-call | flops 4000000000 | bytes 4000000 | tf_op jit(solution)/shard_map/apply_factor/pallas_call | solution.py:227
  108.3 0.9 copy-done
  109.2 8.2 %trailing_update.1 = f32[256,4096]{1,0:T(8,128)} custom-call(f32[256,4096]{1,0:T(8,128)} %k_ref.1, f32[256,512]{1,0:T(8,128)} %copy-done, f32[4096,512]{1,0:T(8,128)} %all-gather.2.cloned.1.call-done.b_ref), custom_call_target="tpu_custom_call" | custom-call | flops 3221225472 | bytes 16000000 | tf_op jit(solution)/shard_map/trailing_update/pallas_call | solution.py:277
  (23 shorter events, 0.2 us)
Async XLA Ops:
  7.2 12.6 %copy-start.2 = (s32[2]{0:T(128)S(1)}, s32[2]{0:T(128)}, u32[]{:S(2)}) copy-start(s32[2]{0:T(128)} %order_ref.7) | copy-start | bytes 28
  7.2 102.0 %all-gather.2.cloned.1.call-start = ((), (), s32[]{:S(2)}) async-start(), calls=%async_computation | async-start | bytes 8519680 | tf_op jit(solution)/shard_map/all_gather | solution.py:466
  9.3 6.0 %collective-permute-start.12 = (f32[64,512]{1,0:T(8,128)S(1)}, f32[64,512]{1,0:T(8,128)S(1)}, u32[]{:S(2)}, u32[]{:S(2)}) collective-permute-start(f32[64,512]{1,0:T(8,128)S(1)} %get-tuple-element.41), channel_id=1, source_target_pairs={{0,1},{1,2},{2,3},{3,0},{4,5},{5,6},{6,7},{7,4},{8,9},{9,10},{10,1... | collective-permute-start | bytes 393224 | tf_op jit(solution)/shard_map/ppermute | solution.py:446
  11.5 8.3 %collective-permute-start.13 = (f32[64,512]{1,0:T(8,128)S(1)}, f32[64,512]{1,0:T(8,128)S(1)}, u32[]{:S(2)}, u32[]{:S(2)}) collective-permute-start(f32[64,512]{1,0:T(8,128)S(1)} %get-tuple-element.42), channel_id=1, source_target_pairs={{0,2},{1,3},{2,0},{3,1},{4,6},{5,7},{6,4},{7,5},{8,10},{9,11},{10,... | collective-permute-start | bytes 393224 | tf_op jit(solution)/shard_map/ppermute | solution.py:446
  14.1 5.7 %collective-permute-start.14 = (f32[64,512]{1,0:T(8,128)S(1)}, f32[64,512]{1,0:T(8,128)S(1)}, u32[]{:S(2)}, u32[]{:S(2)}) collective-permute-start(f32[64,512]{1,0:T(8,128)S(1)} %get-tuple-element.43), channel_id=1, source_target_pairs={{0,3},{1,0},{2,1},{3,2},{4,7},{5,4},{6,5},{7,6},{8,11},{9,8},{10,9... | collective-permute-start | bytes 393224 | tf_op jit(solution)/shard_map/ppermute | solution.py:446
  21.1 5.1 %collective-permute-start = (f32[32,512]{1,0:T(8,128)S(1)}, f32[32,512]{1,0:T(8,128)S(1)}, u32[]{:S(2)}, u32[]{:S(2)}) collective-permute-start(f32[32,512]{1,0:T(8,128)S(1)} %get-tuple-element.36), channel_id=1, source_target_pairs={{0,1},{1,2},{2,3},{3,0},{4,5},{5,6},{6,7},{7,4},{8,9},{9,10},{10,1... | collective-permute-start | bytes 196616 | tf_op jit(solution)/shard_map/ppermute | solution.py:446
  21.2 5.0 %collective-permute-start.1 = (f32[32,512]{1,0:T(8,128)S(1)}, f32[32,512]{1,0:T(8,128)S(1)}, u32[]{:S(2)}, u32[]{:S(2)}) collective-permute-start(f32[32,512]{1,0:T(8,128)S(1)} %get-tuple-element.37), channel_id=1, source_target_pairs={{0,2},{1,3},{2,0},{3,1},{4,6},{5,7},{6,4},{7,5},{8,10},{9,11},{10,... | collective-permute-start | bytes 196616 | tf_op jit(solution)/shard_map/ppermute | solution.py:446
  23.3 3.5 %collective-permute-start.2 = (f32[32,512]{1,0:T(8,128)S(1)}, f32[32,512]{1,0:T(8,128)S(1)}, u32[]{:S(2)}, u32[]{:S(2)}) collective-permute-start(f32[32,512]{1,0:T(8,128)S(1)} %get-tuple-element.38), channel_id=1, source_target_pairs={{0,3},{1,0},{2,1},{3,2},{4,7},{5,4},{6,5},{7,6},{8,11},{9,8},{10,9... | collective-permute-start | bytes 196616 | tf_op jit(solution)/shard_map/ppermute | solution.py:446
  27.4 7.0 %collective-permute-start.5 = (f32[64,512]{1,0:T(8,128)S(1)}, f32[64,512]{1,0:T(8,128)S(1)}, u32[]{:S(2)}, u32[]{:S(2)}) collective-permute-start(f32[64,512]{1,0:T(8,128)S(1)} %choose_shares.1.refs_0_), channel_id=1, source_target_pairs={{0,192},{4,196},{8,200},{12,204},{16,208},{20,212},{24,216},{28,22... | collective-permute-start | bytes 393224 | tf_op jit(solution)/shard_map/ppermute | solution.py:455
  31.0 5.4 %collective-permute-start.4 = (f32[64,512]{1,0:T(8,128)S(1)}, f32[64,512]{1,0:T(8,128)S(1)}, u32[]{:S(2)}, u32[]{:S(2)}) collective-permute-start(f32[64,512]{1,0:T(8,128)S(1)} %choose_shares.1.refs_0_), channel_id=1, source_target_pairs={{0,128},{4,132},{8,136},{12,140},{16,144},{20,148},{24,152},{28,15... | collective-permute-start | bytes 393224 | tf_op jit(solution)/shard_map/ppermute | solution.py:455
  31.5 6.2 %collective-permute-start.3 = (f32[64,512]{1,0:T(8,128)S(1)}, f32[64,512]{1,0:T(8,128)S(1)}, u32[]{:S(2)}, u32[]{:S(2)}) collective-permute-start(f32[64,512]{1,0:T(8,128)S(1)} %choose_shares.1.refs_0_), channel_id=1, source_target_pairs={{0,64},{4,68},{8,72},{12,76},{16,80},{20,84},{24,88},{28,92},{32,9... | collective-permute-start | bytes 393224 | tf_op jit(solution)/shard_map/ppermute | solution.py:455
  38.3 5.4 %collective-permute-start.6 = (f32[64,512]{1,0:T(8,128)S(1)}, f32[64,512]{1,0:T(8,128)S(1)}, u32[]{:S(2)}, u32[]{:S(2)}) collective-permute-start(f32[64,512]{1,0:T(8,128)S(1)} %choose_along_x.1), channel_id=1, source_target_pairs={{0,16},{4,20},{8,24},{12,28},{16,0},{20,4},{24,8},{28,12},{32,48},... | collective-permute-start | bytes 393224 | tf_op jit(solution)/shard_map/ppermute | solution.py:455
  43.8 10.1 %collective-permute-start.7 = (f32[64,512]{1,0:T(8,128)S(1)}, f32[64,512]{1,0:T(8,128)S(1)}, u32[]{:S(2)}, u32[]{:S(2)}) collective-permute-start(f32[64,512]{1,0:T(8,128)S(1)} %compare_select_fusion), channel_id=1, source_target_pairs={{0,48},{4,52},{8,56},{12,60},{16,32},{20,36},{24,40},{28,44},{32,1... | collective-permute-start | bytes 393224 | tf_op jit(solution)/shard_map/ppermute | solution.py:455
  53.9 5.4 %collective-permute-start.8 = (f32[64,512]{1,0:T(8,128)S(1)}, f32[64,512]{1,0:T(8,128)S(1)}, u32[]{:S(2)}, u32[]{:S(2)}) collective-permute-start(f32[64,512]{1,0:T(8,128)S(1)} %compare_select_fusion.1), channel_id=1, source_target_pairs={{0,8},{4,12},{8,0},{12,4},{16,24},{20,28},{24,16},{28,20},{32,40},... | collective-permute-start | bytes 393224 | tf_op jit(solution)/shard_map/ppermute | solution.py:455
  59.4 7.6 %collective-permute-start.11 = (f32[64,512]{1,0:T(8,128)S(1)}, f32[64,512]{1,0:T(8,128)S(1)}, u32[]{:S(2)}, u32[]{:S(2)}) collective-permute-start(f32[64,512]{1,0:T(8,128)S(1)} %pad_maximum_fusion), channel_id=1, source_target_pairs={{0,3},{1,0},{2,1},{3,2},{4,7},{5,4},{6,5},{7,6},{8,11},{9,8},{10,9... | collective-permute-start | bytes 393224 | tf_op jit(solution)/shard_map/ppermute | solution.py:446
  60.2 6.7 %collective-permute-start.10 = (f32[64,512]{1,0:T(8,128)S(1)}, f32[64,512]{1,0:T(8,128)S(1)}, u32[]{:S(2)}, u32[]{:S(2)}) collective-permute-start(f32[64,512]{1,0:T(8,128)S(1)} %pad_maximum_fusion), channel_id=1, source_target_pairs={{0,2},{1,3},{2,0},{3,1},{4,6},{5,7},{6,4},{7,5},{8,10},{9,11},{10,... | collective-permute-start | bytes 393224 | tf_op jit(solution)/shard_map/ppermute | solution.py:446
  61.0 5.9 %collective-permute-start.9 = (f32[64,512]{1,0:T(8,128)S(1)}, f32[64,512]{1,0:T(8,128)S(1)}, u32[]{:S(2)}, u32[]{:S(2)}) collective-permute-start(f32[64,512]{1,0:T(8,128)S(1)} %pad_maximum_fusion), channel_id=1, source_target_pairs={{0,1},{1,2},{2,3},{3,0},{4,5},{5,6},{6,7},{7,4},{8,9},{9,10},{10,1... | collective-permute-start | bytes 393224 | tf_op jit(solution)/shard_map/ppermute | solution.py:446
  67.1 13.4 %collective-permute-start.15 = (f32[320,512]{1,0:T(8,128)S(1)}, f32[320,512]{1,0:T(8,128)S(1)}, u32[]{:S(2)}, u32[]{:S(2)}) collective-permute-start(f32[320,512]{1,0:T(8,128)S(1)} %slice_dynamic-update-slice_fusion.own_ref), channel_id=1, source_target_pairs={{0,4},{4,0},{8,12},{12,8},{16,20},{20,16},{24,28},{28,24},{32,36},... | collective-permute-start | bytes 1966088 | tf_op jit(solution)/shard_map/ppermute | solution.py:455
  78.8 13.2 %collective-permute-start.18 = (f32[64,512]{1,0:T(8,128)}, f32[64,512]{1,0:T(8,128)S(1)}, u32[]{:S(2)}, u32[]{:S(2)}) collective-permute-start(f32[64,512]{1,0:T(8,128)} %choose_pieces.1.refs_0_), channel_id=1, source_target_pairs={{0,3},{1,0},{2,1},{3,2},{4,7},{5,4},{6,5},{7,6},{8,11},{9,8},{10,9... | collective-permute-start | bytes 393224 | tf_op jit(solution)/shard_map/ppermute | solution.py:446
  79.1 12.9 %collective-permute-start.17 = (f32[64,512]{1,0:T(8,128)}, f32[64,512]{1,0:T(8,128)S(1)}, u32[]{:S(2)}, u32[]{:S(2)}) collective-permute-start(f32[64,512]{1,0:T(8,128)} %choose_pieces.1.refs_0_), channel_id=1, source_target_pairs={{0,2},{1,3},{2,0},{3,1},{4,6},{5,7},{6,4},{7,5},{8,10},{9,11},{10,... | collective-permute-start | bytes 393224 | tf_op jit(solution)/shard_map/ppermute | solution.py:446
  79.1 12.8 %collective-permute-start.16 = (f32[64,512]{1,0:T(8,128)}, f32[64,512]{1,0:T(8,128)S(1)}, u32[]{:S(2)}, u32[]{:S(2)}) collective-permute-start(f32[64,512]{1,0:T(8,128)} %choose_pieces.1.refs_0_), channel_id=1, source_target_pairs={{0,1},{1,2},{2,3},{3,0},{4,5},{5,6},{6,7},{7,4},{8,9},{9,10},{10,1... | collective-permute-start | bytes 393224 | tf_op jit(solution)/shard_map/ppermute | solution.py:446
  92.0 10.8 %copy-start.1 = (f32[256,128]{1,0:T(8,128)S(1)}, f32[256,128]{1,0:T(8,128)}, u32[]{:S(2)}) copy-start(f32[256,128]{1,0:T(8,128)} %refs_8_.1) | copy-start | bytes 393220
  92.0 10.8 %copy-start.3 = (s32[4]{0:T(128)S(1)}, s32[4]{0:T(128)}, u32[]{:S(2)}) copy-start(s32[4]{0:T(128)} %block_ref.3) | copy-start | bytes 52
  108.3 0.9 copy-start
Sparse Core Ops, SparseCore 0:
  21.2 86.8 all-gather.1

commit v2 on v1

--- a/solution.py
+++ b/solution.py
@@ -292,7 +292,7 @@
             pltpu.SemaphoreType.DMA((count,)),
         ],
         cost_estimate=pl.CostEstimate(flops=6 * rows * cols * size, bytes_accessed=16_000_000, transcendentals=0),
-        compiler_params=pltpu.CompilerParams(vmem_limit_bytes=54 * 1024 * 1024),
+        compiler_params=pltpu.CompilerParams(vmem_limit_bytes=50 * 1024 * 1024),
         name="trailing_update",
     )(kernel, weights, across)
 

time: 124 us -> 122 us (0.984)
  transfers between devices with their start and end apart: 20 -> 20, of which waited for: 12 -> 12; matrix products, arithmetic and copies ran while one was open for 0% -> 0% of each run, Pallas kernels for 23% -> 24%
where the time goes in v2:
time: 122 us
  starting transfers between devices  41.7 us (34%)
  Pallas kernels  39.2 us (32%)
  waiting for transfers between devices  26.8 us (22%)
  between operations  14.3 us (12%)
    ppermute x7, starting transfers between devices, along_rows(): return lax.ppermute(array, 'rows', pairs)  28 us
    ppermute x7, waiting for transfers between devices, along_rows(): return lax.ppermute(array, 'rows', pairs)  15.2 us
    ppermute x12, starting transfers between devices, along_y(): lax.ppermute(array, 'cols', [(i, (i + shift) % cols_count) for i in range...  13.6 us
    ppermute x12, waiting for transfers between devices, along_y(): lax.ppermute(array, 'cols', [(i, (i + shift) % cols_count) for i in range...  11.7 us
    pallas_call x1, Pallas kernels, first_call(): pl.pallas_call(first_kernel, out_shape=[square(PW), square(PW), square(PW...  11.4 us
    pallas_call x1, Pallas kernels, second_call(): pl.pallas_call(second_kernel, out_shape=[square(PW), square(PW)], scratch...  10.8 us
    pallas_call x1, Pallas kernels, update_call(): pl.pallas_call(update_kernel, in_specs=[pl.BlockSpec(memory_space=pltpu.H...  7.12 us
    pallas_call x1, Pallas kernels, apply_call(): pl.pallas_call(apply_kernel, in_specs=[pl.BlockSpec(memory_space=pltpu.SM...  5.41 us
  transfers between devices with their start and end apart: 20, of which 12 were waited for; matrix products, arithmetic and copies ran while one was open for 0% of the time, Pallas kernels for 24%

profile of v2, /device:TPU:1, one launch (start us, length us, event | category | flops | bytes accessed | tf_op | source)
XLA Modules:
  0.0 122.2 jit_solution(14838951945306113412)
XLA Ops:
  7.2 0.0 all-gather.2.cloned.1.call-start
  7.2 2.0 %pack_messages.1 = (f32[64,512]{1,0:T(8,128)S(1)}, f32[64,512]{1,0:T(8,128)S(1)}, f32[64,512]{1,0:T(8,128)S(1)}, f32[64,512]{1,0:T(8,128)S(1)}, f32[32,512]{1,0:...) custom-call(s32[2]{0:T(128)} %order_ref.7, ...), custom_call_target="tpu_custom_call" | custom-call | bytes 2000000 | tf_op jit(solution)/shard_map/pack_messages/pallas_call | solution.py:357
  9.3 2.2 %collective-permute-start.12 = (f32[64,512]{1,0:T(8,128)S(1)}, f32[64,512]{1,0:T(8,128)S(1)}, u32[]{:S(2)}, u32[]{:S(2)}) collective-permute-start(f32[64,512]{1,0:T(8,128)S(1)} %get-tuple-element.41), channel_id=1, source_target_pairs={{0,1},{1,2},{2,3},{3,0},{4,5},{5,6},{6,7},{7,4},{8,9},{9,10},{10,1... | collective-permute-start | bytes 393224 | tf_op jit(solution)/shard_map/ppermute | solution.py:446
  11.5 2.6 %collective-permute-start.13 = (f32[64,512]{1,0:T(8,128)S(1)}, f32[64,512]{1,0:T(8,128)S(1)}, u32[]{:S(2)}, u32[]{:S(2)}) collective-permute-start(f32[64,512]{1,0:T(8,128)S(1)} %get-tuple-element.42), channel_id=1, source_target_pairs={{0,2},{1,3},{2,0},{3,1},{4,6},{5,7},{6,4},{7,5},{8,10},{9,11},{10,... | collective-permute-start | bytes 393224 | tf_op jit(solution)/shard_map/ppermute | solution.py:446
  14.1 1.1 collective-permute-start.14
  15.2 0.1 collective-permute-done.12.refs_1_
  15.3 4.5 %collective-permute-done.13.refs_2_ = f32[64,512]{1,0:T(8,128)S(1)} collective-permute-done((f32[64,512]{1,0:T(8,128)S(1)}, f32[64,512]{1,0:T(8,128)S(1)}, u32[]{:S(2)}, u32[]{:S(2)}) %collective-permute-start.13) | collective-permute-done | bytes 131104 | tf_op jit(solution)/shard_map/ppermute | solution.py:446
  19.8 0.0 collective-permute-done.14.refs_3_
  19.8 1.3 %choose_pieces.1.refs_0_ = f32[64,512]{1,0:T(8,128)} custom-call(s32[2]{0:T(128)S(1)} %copy-done.1, f32[64,512]{1,0:T(8,128)S(1)} %get-tuple-element.40.refs_0_, f32[64,512]{1,0:T(8,128)S(1)} %collective-permute-done.12.refs_1_, f32[64,512]{1,0:T(8,128)S(1)} %collective-permute-done.13.refs_2_, f32[64,512]{1,0:T(8,128)S(1)} %collective-permute-done.14.refs_3_), custom_call_target="tpu_custom_call" | custom-call | bytes 1000000 | tf_op jit(solution)/shard_map/choose_pieces/pallas_call | solution.py:430
  21.0 0.0 all-gather.2.cloned.1.call-update
  21.1 0.1 collective-permute-start
  21.2 2.1 %collective-permute-start.1 = (f32[32,512]{1,0:T(8,128)S(1)}, f32[32,512]{1,0:T(8,128)S(1)}, u32[]{:S(2)}, u32[]{:S(2)}) collective-permute-start(f32[32,512]{1,0:T(8,128)S(1)} %get-tuple-element.37), channel_id=1, source_target_pairs={{0,2},{1,3},{2,0},{3,1},{4,6},{5,7},{6,4},{7,5},{8,10},{9,11},{10,... | collective-permute-start | bytes 196616 | tf_op jit(solution)/shard_map/ppermute | solution.py:446
  23.3 1.7 %collective-permute-start.2 = (f32[32,512]{1,0:T(8,128)S(1)}, f32[32,512]{1,0:T(8,128)S(1)}, u32[]{:S(2)}, u32[]{:S(2)}) collective-permute-start(f32[32,512]{1,0:T(8,128)S(1)} %get-tuple-element.38), channel_id=1, source_target_pairs={{0,3},{1,0},{2,1},{3,2},{4,7},{5,4},{6,5},{7,6},{8,11},{9,8},{10,9... | collective-permute-start | bytes 196616 | tf_op jit(solution)/shard_map/ppermute | solution.py:446
  24.9 1.2 %collective-permute-done.refs_1_ = f32[32,512]{1,0:T(8,128)S(1)} collective-permute-done((f32[32,512]{1,0:T(8,128)S(1)}, f32[32,512]{1,0:T(8,128)S(1)}, u32[]{:S(2)}, u32[]{:S(2)}) %collective-permute-start) | collective-permute-done | bytes 65568 | tf_op jit(solution)/shard_map/ppermute | solution.py:446
  26.2 0.0 collective-permute-done.1.refs_2_
  26.2 0.6 collective-permute-done.2.refs_3_
  26.8 0.6 choose_shares.1.refs_0_
  27.4 3.6 %collective-permute-start.5 = (f32[64,512]{1,0:T(8,128)S(1)}, f32[64,512]{1,0:T(8,128)S(1)}, u32[]{:S(2)}, u32[]{:S(2)}) collective-permute-start(f32[64,512]{1,0:T(8,128)S(1)} %choose_shares.1.refs_0_), channel_id=1, source_target_pairs={{0,192},{4,196},{8,200},{12,204},{16,208},{20,212},{24,216},{28,22... | collective-permute-start | bytes 393224 | tf_op jit(solution)/shard_map/ppermute | solution.py:455
  31.0 0.5 collective-permute-start.4
  31.5 0.6 collective-permute-start.3
  32.1 2.2 %collective-permute-done.5.refs_3_ = f32[64,512]{1,0:T(8,128)S(1)} collective-permute-done((f32[64,512]{1,0:T(8,128)S(1)}, f32[64,512]{1,0:T(8,128)S(1)}, u32[]{:S(2)}, u32[]{:S(2)}) %collective-permute-start.5) | collective-permute-done | bytes 131104 | tf_op jit(solution)/shard_map/ppermute | solution.py:455
  34.3 2.1 %collective-permute-done.4.refs_2_ = f32[64,512]{1,0:T(8,128)S(1)} collective-permute-done((f32[64,512]{1,0:T(8,128)S(1)}, f32[64,512]{1,0:T(8,128)S(1)}, u32[]{:S(2)}, u32[]{:S(2)}) %collective-permute-start.4) | collective-permute-done | bytes 131104 | tf_op jit(solution)/shard_map/ppermute | solution.py:455
  36.4 1.3 %collective-permute-done.3.refs_1_ = f32[64,512]{1,0:T(8,128)S(1)} collective-permute-done((f32[64,512]{1,0:T(8,128)S(1)}, f32[64,512]{1,0:T(8,128)S(1)}, u32[]{:S(2)}, u32[]{:S(2)}) %collective-permute-start.3) | collective-permute-done | bytes 131104 | tf_op jit(solution)/shard_map/ppermute | solution.py:455
  37.7 0.6 choose_along_x.1
  38.3 3.1 %collective-permute-start.6 = (f32[64,512]{1,0:T(8,128)S(1)}, f32[64,512]{1,0:T(8,128)S(1)}, u32[]{:S(2)}, u32[]{:S(2)}) collective-permute-start(f32[64,512]{1,0:T(8,128)S(1)} %choose_along_x.1), channel_id=1, source_target_pairs={{0,16},{4,20},{8,24},{12,28},{16,0},{20,4},{24,8},{28,12},{32,48},... | collective-permute-start | bytes 393224 | tf_op jit(solution)/shard_map/ppermute | solution.py:455
  41.4 2.4 %collective-permute-done.6 = f32[64,512]{1,0:T(8,128)S(1)} collective-permute-done((f32[64,512]{1,0:T(8,128)S(1)}, f32[64,512]{1,0:T(8,128)S(1)}, u32[]{:S(2)}, u32[]{:S(2)}) %collective-permute-start.6) | collective-permute-done | bytes 131104 | tf_op jit(solution)/shard_map/ppermute | solution.py:455
  43.8 6.3 %collective-permute-start.7 = (f32[64,512]{1,0:T(8,128)S(1)}, f32[64,512]{1,0:T(8,128)S(1)}, u32[]{:S(2)}, u32[]{:S(2)}) collective-permute-start(f32[64,512]{1,0:T(8,128)S(1)} %compare_select_fusion), channel_id=1, source_target_pairs={{0,48},{4,52},{8,56},{12,60},{16,32},{20,36},{24,40},{28,44},{32,1... | collective-permute-start | bytes 393224 | tf_op jit(solution)/shard_map/ppermute | solution.py:455
  50.1 3.8 %collective-permute-done.7 = f32[64,512]{1,0:T(8,128)S(1)} collective-permute-done((f32[64,512]{1,0:T(8,128)S(1)}, f32[64,512]{1,0:T(8,128)S(1)}, u32[]{:S(2)}, u32[]{:S(2)}) %collective-permute-start.7) | collective-permute-done | bytes 131104 | tf_op jit(solution)/shard_map/ppermute | solution.py:455
  53.9 2.2 %collective-permute-start.8 = (f32[64,512]{1,0:T(8,128)S(1)}, f32[64,512]{1,0:T(8,128)S(1)}, u32[]{:S(2)}, u32[]{:S(2)}) collective-permute-start(f32[64,512]{1,0:T(8,128)S(1)} %compare_select_fusion.1), channel_id=1, source_target_pairs={{0,8},{4,12},{8,0},{12,4},{16,24},{20,28},{24,16},{28,20},{32,40},... | collective-permute-start | bytes 393224 | tf_op jit(solution)/shard_map/ppermute | solution.py:455
  56.2 3.1 %collective-permute-done.8 = f32[64,512]{1,0:T(8,128)S(1)} collective-permute-done((f32[64,512]{1,0:T(8,128)S(1)}, f32[64,512]{1,0:T(8,128)S(1)}, u32[]{:S(2)}, u32[]{:S(2)}) %collective-permute-start.8) | collective-permute-done | bytes 131104 | tf_op jit(solution)/shard_map/ppermute | solution.py:455
  59.4 0.9 collective-permute-start.11
  60.2 0.8 collective-permute-start.10
  61.0 0.7 collective-permute-start.9
  61.8 5.2 %collective-permute-done.9 = f32[64,512]{1,0:T(8,128)S(1)} collective-permute-done((f32[64,512]{1,0:T(8,128)S(1)}, f32[64,512]{1,0:T(8,128)S(1)}, u32[]{:S(2)}, u32[]{:S(2)}) %collective-permute-start.9) | collective-permute-done | bytes 131104 | tf_op jit(solution)/shard_map/ppermute | solution.py:446
  67.0 0.0 collective-permute-done.10
  67.1 11.7 %collective-permute-start.15 = (f32[320,512]{1,0:T(8,128)S(1)}, f32[320,512]{1,0:T(8,128)S(1)}, u32[]{:S(2)}, u32[]{:S(2)}) collective-permute-start(f32[320,512]{1,0:T(8,128)S(1)} %slice_dynamic-update-slice_fusion.own_ref), channel_id=1, source_target_pairs={{0,4},{4,0},{8,12},{12,8},{16,20},{20,16},{24,28},{28,24},{32,36},... | collective-permute-start | bytes 1966088 | tf_op jit(solution)/shard_map/ppermute | solution.py:455
  78.8 0.3 collective-permute-start.18
  79.1 0.1 collective-permute-start.17
  79.1 1.1 collective-permute-start.16
  80.2 0.2 collective-permute-done.15.other_ref
  80.5 11.4 %eliminate_first.1 = (f32[256,256]{1,0:T(8,128)S(1)}, f32[256,256]{1,0:T(8,128)S(1)}, f32[256,256]{1,0:T(8,128)S(1)}, f32[512,128]{1,0:T(8,128)S(1)}) custom-call(f32[320,512]{1,0:T(8,128)S(1)} %slice_dynamic-update-slice_fusion.own_ref, f32[320,512]{1,0:T(8,128)S(1)} %collective-permute-done.15.other_ref), custom_call_target="tpu_custom_call" | custom-call | flops 12000000000 | bytes 2000000 | tf_op jit(solution)/shard_map/eliminate_first/pallas_call | solution.py:158
  91.9 0.0 collective-permute-done.17.refs_2_
  92.0 0.0 collective-permute-done.16.refs_1_
  92.0 0.0 copy-start
  92.0 0.0 copy-start.2
  92.0 10.8 %eliminate_second.1 = (f32[256,256]{1,0:T(8,128)S(1)}, f32[256,256]{1,0:T(8,128)S(1)}) custom-call(f32[256,256]{1,0:T(8,128)S(1)} %get-tuple-element.53.rest_ref, f32[256,256]{1,0:T(8,128)S(1)} %get-tuple-element.54.under_ref), custom_call_target="tpu_custom_call" | custom-call | flops 12000000000 | bytes 2000000 | tf_op jit(solution)/shard_map/eliminate_second/pallas_call | solution.py:180
  102.8 5.4 %apply_factor.1 = (f32[256,512]{1,0:T(8,128)}, f32[256,512]{1,0:T(8,128)S(1)}, f32[512,128]{1,0:T(8,128)}, f32[256,128]{1,0:T(8,128)}) custom-call(s32[4]{0:T(128)S(1)} %copy-done.2, f32[64,512]{1,0:T(8,128)} %choose_pieces.1.refs_0_, f32[64,512]{1,0:T(8,128)S(1)} %collective-permute-done.16.refs_1_, f32[64,512]{1,0:T(8,128)S(1)} %collective-permute-done.17.refs_2_, ...), custom_call_target="tpu_custom_call" | custom-call | flops 4000000000 | bytes 4000000 | tf_op jit(solution)/shard_map/apply_factor/pallas_call | solution.py:227
  108.2 7.1 %trailing_update.1 = f32[256,4096]{1,0:T(8,128)} custom-call(f32[256,4096]{1,0:T(8,128)} %k_ref.1, f32[256,512]{1,0:T(8,128)S(1)} %get-tuple-element.58.w_ref, f32[4096,512]{1,0:T(8,128)} %all-gather.2.cloned.1.call-done.b_ref), custom_call_target="tpu_custom_call" | custom-call | flops 3221225472 | bytes 16000000 | tf_op jit(solution)/shard_map/trailing_update/pallas_call | solution.py:277
  (21 shorter events, 0.2 us)
Async XLA Ops:
  7.2 12.6 %copy-start.1 = (s32[2]{0:T(128)S(1)}, s32[2]{0:T(128)}, u32[]{:S(2)}) copy-start(s32[2]{0:T(128)} %order_ref.7) | copy-start | bytes 28
  7.2 101.1 %all-gather.2.cloned.1.call-start = ((), (), s32[]{:S(2)}) async-start(), calls=%async_computation | async-start | bytes 8519680 | tf_op jit(solution)/shard_map/all_gather | solution.py:466
  9.3 6.0 %collective-permute-start.12 = (f32[64,512]{1,0:T(8,128)S(1)}, f32[64,512]{1,0:T(8,128)S(1)}, u32[]{:S(2)}, u32[]{:S(2)}) collective-permute-start(f32[64,512]{1,0:T(8,128)S(1)} %get-tuple-element.41), channel_id=1, source_target_pairs={{0,1},{1,2},{2,3},{3,0},{4,5},{5,6},{6,7},{7,4},{8,9},{9,10},{10,1... | collective-permute-start | bytes 393224 | tf_op jit(solution)/shard_map/ppermute | solution.py:446
  11.5 8.3 %collective-permute-start.13 = (f32[64,512]{1,0:T(8,128)S(1)}, f32[64,512]{1,0:T(8,128)S(1)}, u32[]{:S(2)}, u32[]{:S(2)}) collective-permute-start(f32[64,512]{1,0:T(8,128)S(1)} %get-tuple-element.42), channel_id=1, source_target_pairs={{0,2},{1,3},{2,0},{3,1},{4,6},{5,7},{6,4},{7,5},{8,10},{9,11},{10,... | collective-permute-start | bytes 393224 | tf_op jit(solution)/shard_map/ppermute | solution.py:446
  14.1 5.7 %collective-permute-start.14 = (f32[64,512]{1,0:T(8,128)S(1)}, f32[64,512]{1,0:T(8,128)S(1)}, u32[]{:S(2)}, u32[]{:S(2)}) collective-permute-start(f32[64,512]{1,0:T(8,128)S(1)} %get-tuple-element.43), channel_id=1, source_target_pairs={{0,3},{1,0},{2,1},{3,2},{4,7},{5,4},{6,5},{7,6},{8,11},{9,8},{10,9... | collective-permute-start | bytes 393224 | tf_op jit(solution)/shard_map/ppermute | solution.py:446
  21.1 5.1 %collective-permute-start = (f32[32,512]{1,0:T(8,128)S(1)}, f32[32,512]{1,0:T(8,128)S(1)}, u32[]{:S(2)}, u32[]{:S(2)}) collective-permute-start(f32[32,512]{1,0:T(8,128)S(1)} %get-tuple-element.36), channel_id=1, source_target_pairs={{0,1},{1,2},{2,3},{3,0},{4,5},{5,6},{6,7},{7,4},{8,9},{9,10},{10,1... | collective-permute-start | bytes 196616 | tf_op jit(solution)/shard_map/ppermute | solution.py:446
  21.2 5.0 %collective-permute-start.1 = (f32[32,512]{1,0:T(8,128)S(1)}, f32[32,512]{1,0:T(8,128)S(1)}, u32[]{:S(2)}, u32[]{:S(2)}) collective-permute-start(f32[32,512]{1,0:T(8,128)S(1)} %get-tuple-element.37), channel_id=1, source_target_pairs={{0,2},{1,3},{2,0},{3,1},{4,6},{5,7},{6,4},{7,5},{8,10},{9,11},{10,... | collective-permute-start | bytes 196616 | tf_op jit(solution)/shard_map/ppermute | solution.py:446
  23.3 3.5 %collective-permute-start.2 = (f32[32,512]{1,0:T(8,128)S(1)}, f32[32,512]{1,0:T(8,128)S(1)}, u32[]{:S(2)}, u32[]{:S(2)}) collective-permute-start(f32[32,512]{1,0:T(8,128)S(1)} %get-tuple-element.38), channel_id=1, source_target_pairs={{0,3},{1,0},{2,1},{3,2},{4,7},{5,4},{6,5},{7,6},{8,11},{9,8},{10,9... | collective-permute-start | bytes 196616 | tf_op jit(solution)/shard_map/ppermute | solution.py:446
  27.4 7.0 %collective-permute-start.5 = (f32[64,512]{1,0:T(8,128)S(1)}, f32[64,512]{1,0:T(8,128)S(1)}, u32[]{:S(2)}, u32[]{:S(2)}) collective-permute-start(f32[64,512]{1,0:T(8,128)S(1)} %choose_shares.1.refs_0_), channel_id=1, source_target_pairs={{0,192},{4,196},{8,200},{12,204},{16,208},{20,212},{24,216},{28,22... | collective-permute-start | bytes 393224 | tf_op jit(solution)/shard_map/ppermute | solution.py:455
  31.0 5.4 %collective-permute-start.4 = (f32[64,512]{1,0:T(8,128)S(1)}, f32[64,512]{1,0:T(8,128)S(1)}, u32[]{:S(2)}, u32[]{:S(2)}) collective-permute-start(f32[64,512]{1,0:T(8,128)S(1)} %choose_shares.1.refs_0_), channel_id=1, source_target_pairs={{0,128},{4,132},{8,136},{12,140},{16,144},{20,148},{24,152},{28,15... | collective-permute-start | bytes 393224 | tf_op jit(solution)/shard_map/ppermute | solution.py:455
  31.5 6.2 %collective-permute-start.3 = (f32[64,512]{1,0:T(8,128)S(1)}, f32[64,512]{1,0:T(8,128)S(1)}, u32[]{:S(2)}, u32[]{:S(2)}) collective-permute-start(f32[64,512]{1,0:T(8,128)S(1)} %choose_shares.1.refs_0_), channel_id=1, source_target_pairs={{0,64},{4,68},{8,72},{12,76},{16,80},{20,84},{24,88},{28,92},{32,9... | collective-permute-start | bytes 393224 | tf_op jit(solution)/shard_map/ppermute | solution.py:455
  38.3 5.4 %collective-permute-start.6 = (f32[64,512]{1,0:T(8,128)S(1)}, f32[64,512]{1,0:T(8,128)S(1)}, u32[]{:S(2)}, u32[]{:S(2)}) collective-permute-start(f32[64,512]{1,0:T(8,128)S(1)} %choose_along_x.1), channel_id=1, source_target_pairs={{0,16},{4,20},{8,24},{12,28},{16,0},{20,4},{24,8},{28,12},{32,48},... | collective-permute-start | bytes 393224 | tf_op jit(solution)/shard_map/ppermute | solution.py:455
  43.8 10.1 %collective-permute-start.7 = (f32[64,512]{1,0:T(8,128)S(1)}, f32[64,512]{1,0:T(8,128)S(1)}, u32[]{:S(2)}, u32[]{:S(2)}) collective-permute-start(f32[64,512]{1,0:T(8,128)S(1)} %compare_select_fusion), channel_id=1, source_target_pairs={{0,48},{4,52},{8,56},{12,60},{16,32},{20,36},{24,40},{28,44},{32,1... | collective-permute-start | bytes 393224 | tf_op jit(solution)/shard_map/ppermute | solution.py:455
  53.9 5.4 %collective-permute-start.8 = (f32[64,512]{1,0:T(8,128)S(1)}, f32[64,512]{1,0:T(8,128)S(1)}, u32[]{:S(2)}, u32[]{:S(2)}) collective-permute-start(f32[64,512]{1,0:T(8,128)S(1)} %compare_select_fusion.1), channel_id=1, source_target_pairs={{0,8},{4,12},{8,0},{12,4},{16,24},{20,28},{24,16},{28,20},{32,40},... | collective-permute-start | bytes 393224 | tf_op jit(solution)/shard_map/ppermute | solution.py:455
  59.4 7.6 %collective-permute-start.11 = (f32[64,512]{1,0:T(8,128)S(1)}, f32[64,512]{1,0:T(8,128)S(1)}, u32[]{:S(2)}, u32[]{:S(2)}) collective-permute-start(f32[64,512]{1,0:T(8,128)S(1)} %pad_maximum_fusion), channel_id=1, source_target_pairs={{0,3},{1,0},{2,1},{3,2},{4,7},{5,4},{6,5},{7,6},{8,11},{9,8},{10,9... | collective-permute-start | bytes 393224 | tf_op jit(solution)/shard_map/ppermute | solution.py:446
  60.2 6.7 %collective-permute-start.10 = (f32[64,512]{1,0:T(8,128)S(1)}, f32[64,512]{1,0:T(8,128)S(1)}, u32[]{:S(2)}, u32[]{:S(2)}) collective-permute-start(f32[64,512]{1,0:T(8,128)S(1)} %pad_maximum_fusion), channel_id=1, source_target_pairs={{0,2},{1,3},{2,0},{3,1},{4,6},{5,7},{6,4},{7,5},{8,10},{9,11},{10,... | collective-permute-start | bytes 393224 | tf_op jit(solution)/shard_map/ppermute | solution.py:446
  61.0 5.9 %collective-permute-start.9 = (f32[64,512]{1,0:T(8,128)S(1)}, f32[64,512]{1,0:T(8,128)S(1)}, u32[]{:S(2)}, u32[]{:S(2)}) collective-permute-start(f32[64,512]{1,0:T(8,128)S(1)} %pad_maximum_fusion), channel_id=1, source_target_pairs={{0,1},{1,2},{2,3},{3,0},{4,5},{5,6},{6,7},{7,4},{8,9},{9,10},{10,1... | collective-permute-start | bytes 393224 | tf_op jit(solution)/shard_map/ppermute | solution.py:446
  67.1 13.4 %collective-permute-start.15 = (f32[320,512]{1,0:T(8,128)S(1)}, f32[320,512]{1,0:T(8,128)S(1)}, u32[]{:S(2)}, u32[]{:S(2)}) collective-permute-start(f32[320,512]{1,0:T(8,128)S(1)} %slice_dynamic-update-slice_fusion.own_ref), channel_id=1, source_target_pairs={{0,4},{4,0},{8,12},{12,8},{16,20},{20,16},{24,28},{28,24},{32,36},... | collective-permute-start | bytes 1966088 | tf_op jit(solution)/shard_map/ppermute | solution.py:455
  78.8 13.2 %collective-permute-start.18 = (f32[64,512]{1,0:T(8,128)}, f32[64,512]{1,0:T(8,128)S(1)}, u32[]{:S(2)}, u32[]{:S(2)}) collective-permute-start(f32[64,512]{1,0:T(8,128)} %choose_pieces.1.refs_0_), channel_id=1, source_target_pairs={{0,3},{1,0},{2,1},{3,2},{4,7},{5,4},{6,5},{7,6},{8,11},{9,8},{10,9... | collective-permute-start | bytes 393224 | tf_op jit(solution)/shard_map/ppermute | solution.py:446
  79.1 12.9 %collective-permute-start.17 = (f32[64,512]{1,0:T(8,128)}, f32[64,512]{1,0:T(8,128)S(1)}, u32[]{:S(2)}, u32[]{:S(2)}) collective-permute-start(f32[64,512]{1,0:T(8,128)} %choose_pieces.1.refs_0_), channel_id=1, source_target_pairs={{0,2},{1,3},{2,0},{3,1},{4,6},{5,7},{6,4},{7,5},{8,10},{9,11},{10,... | collective-permute-start | bytes 393224 | tf_op jit(solution)/shard_map/ppermute | solution.py:446
  79.1 12.8 %collective-permute-start.16 = (f32[64,512]{1,0:T(8,128)}, f32[64,512]{1,0:T(8,128)S(1)}, u32[]{:S(2)}, u32[]{:S(2)}) collective-permute-start(f32[64,512]{1,0:T(8,128)} %choose_pieces.1.refs_0_), channel_id=1, source_target_pairs={{0,1},{1,2},{2,3},{3,0},{4,5},{5,6},{6,7},{7,4},{8,9},{9,10},{10,1... | collective-permute-start | bytes 393224 | tf_op jit(solution)/shard_map/ppermute | solution.py:446
  92.0 10.8 %copy-start = (f32[256,128]{1,0:T(8,128)S(1)}, f32[256,128]{1,0:T(8,128)}, u32[]{:S(2)}) copy-start(f32[256,128]{1,0:T(8,128)} %refs_8_.1) | copy-start | bytes 393220
  92.0 10.8 %copy-start.2 = (s32[4]{0:T(128)S(1)}, s32[4]{0:T(128)}, u32[]{:S(2)}) copy-start(s32[4]{0:T(128)} %block_ref.3) | copy-start | bytes 52
Sparse Core Ops, SparseCore 0:
  21.2 86.9 all-gather.1

commit v3 on v2

--- a/solution.py
+++ b/solution.py
@@ -95,7 +95,7 @@
     return high, (array - high.astype(jnp.float32)).astype(jnp.bfloat16)
 
 
-def two_tiles(a, v, d, x):
+def two_tiles(a, v, d, x, beside=None):
     v[...] = jnp.zeros_like(v)
 
     @pl.loop(0, 2)
@@ -103,6 +103,8 @@
         at = pl.multiple_of(k * SIDE, SIDE)
         d[...] = a[pl.ds(at, SIDE), pl.ds(at, SIDE)]
         tile_inverse(d, x)
+        if beside is not None:
+            beside(at)
 
         @pl.when(k == 0)
         def _():
@@ -170,29 +172,9 @@
     )(own, other)
 
 
-def second_kernel(rest_ref, under_ref, v_ref, cross_ref, a, d, x):
-    a[...] = rest_ref[...]
-    two_tiles(a, v_ref, d, x)
-    cross_ref[...] = dot_nn(v_ref[...], under_ref[...])
-
-
-def second_call(rest, under):
-    return pl.pallas_call(
-        second_kernel,
-        out_shape=[square(PW), square(PW)],
-        scratch_shapes=[
-            pltpu.VMEM((PW, PW), jnp.float32),
-            pltpu.VMEM((SIDE, SIDE), jnp.float32),
-            pltpu.VMEM((SIDE, SIDE), jnp.float32),
-        ],
-        cost_estimate=pl.CostEstimate(flops=12_000_000_000, bytes_accessed=2_000_000, transcendentals=0),
-        compiler_params=pltpu.CompilerParams(vmem_limit_bytes=16 * 1024 * 1024),
-        name="eliminate_second",
-    )(rest, under)
-
-
-def apply_kernel(block_ref, *refs):
-    pieces, (v1_ref, cross_ref, v2_ref, rc_ref, ri_ref, f_ref, w_ref, y_ref, r_ref, p) = refs[:-10], refs[-10:]
+def second_kernel(block_ref, *refs):
+    pieces, refs = refs[:-16], refs[-16:]
+    v1_ref, rest_ref, under_ref, rc_ref, ri_ref, f_ref, w_ref, y_ref, r_ref, a, v2_ref, d, x, p, t, s_ref = refs
     me = lax.axis_index("cols")
     rows_count = lax.axis_size("rows")
     block_rows = pieces[0].shape[0]
@@ -204,28 +186,36 @@
             def _():
                 p[u * block_rows : (u + 1) * block_rows] = piece[...]
 
-    v1, cross, v2 = v1_ref[...], cross_ref[...], v2_ref[...]
-    p1, p2 = p[:, :PW], p[:, PW:]
-    f1 = dot_nt(p1, v1)
-    f2 = dot_nt(p1, cross) + dot_nt(p2, v2)
-    f_ref[:, :PW] = f1
+    def beside(at):
+        rows = pl.ds(at, SIDE)
+        p1, v1 = p[rows, :PW], v1_ref[...]
+        f1 = dot_nt(p1, v1)
+        f_ref[rows, :PW] = f1
+        w_ref[rows, :PW] = dot_nn(f1, v1)
+        t[rows, :] = p[rows, PW:] + dot_nt(p1, under_ref[...])
+        y_ref[rows, :] = dot_nn(v1_ref[rows, :], rc_ref[:PW])
+        s_ref[rows, :] = rc_ref[pl.ds(PW + at, SIDE), :] + dot_nn(under_ref[rows, :], rc_ref[:PW])
+
+    a[...] = rest_ref[...]
+    two_tiles(a, v2_ref, d, x, beside)
+    v2 = v2_ref[...]
+    f2 = dot_nt(t[...], v2)
     f_ref[:, PW:] = f2
-    w_ref[:, :PW] = dot_nn(f1, v1) + dot_nn(f2, cross)
-    w_ref[:, PW:] = dot_nn(f2, v2)
-    y1 = dot_nn(v1, rc_ref[:PW])
-    y2 = dot_nn(cross, rc_ref[:PW]) + dot_nn(v2, rc_ref[PW:])
-    y_ref[:PW] = y1
+    w2 = dot_nn(f2, v2)
+    w_ref[:, PW:] = w2
+    w_ref[:, :PW] = w_ref[:, :PW] + dot_nn(w2, under_ref[...])
+    y2 = dot_nn(v2, s_ref[...])
     y_ref[PW:] = y2
-    r_ref[...] = ri_ref[...] - dot_nn(f1, y1) - dot_nn(f2, y2)
-
-
-def apply_call(row_block, pieces, v1, cross, v2, rc, ri):
+    r_ref[...] = ri_ref[...] - dot_nn(f_ref[:, :PW], y_ref[:PW]) - dot_nn(f2, y2)
+
+
+def second_call(row_block, pieces, v1, rest, under, rc, ri):
     size, right = rc.shape
     rows = ri.shape[0]
     f32 = jnp.float32
-    operands = (*pieces, v1, cross, v2, rc, ri)
+    operands = (*pieces, v1, rest, under, rc, ri)
     return pl.pallas_call(
-        apply_kernel,
+        second_kernel,
         in_specs=[pl.BlockSpec(memory_space=pltpu.SMEM)]
         + [pl.BlockSpec(memory_space=pltpu.VMEM)] * len(operands),
         out_shape=[
@@ -234,10 +224,18 @@
             jax.ShapeDtypeStruct((size, right), f32),
             jax.ShapeDtypeStruct((rows, right), f32),
         ],
-        scratch_shapes=[pltpu.VMEM((rows, size), f32)],
-        cost_estimate=pl.CostEstimate(flops=4_000_000_000, bytes_accessed=4_000_000, transcendentals=0),
+        scratch_shapes=[
+            pltpu.VMEM((PW, PW), f32),
+            pltpu.VMEM((PW, PW), f32),
+            pltpu.VMEM((SIDE, SIDE), f32),
+            pltpu.VMEM((SIDE, SIDE), f32),
+            pltpu.VMEM((rows, size), f32),
+            pltpu.VMEM((rows, PW), f32),
+            pltpu.VMEM((PW, right), f32),
+        ],
+        cost_estimate=pl.CostEstimate(flops=16_000_000_000, bytes_accessed=4_000_000, transcendentals=0),
         compiler_params=pltpu.CompilerParams(vmem_limit_bytes=16 * 1024 * 1024),
-        name="apply_factor",
+        name="eliminate_second",
     )(row_block, *operands)
 
 
@@ -488,8 +486,7 @@
 
     v1, rest, under, right = first_call(load, other)
     rest, under, *pieces = lax.optimization_barrier((rest, under, *pieces))
-    v2, cross = second_call(rest, under)
-    factor, weights, solved, reduced = apply_call(row_block, pieces, v1, cross, v2, right, samples)
+    factor, weights, solved, reduced = second_call(row_block, pieces, v1, rest, under, right, samples)
     trailing = update_call(kernel, weights, across)
     return trailing, factor, solved, reduced
 

time: 122 us -> 122 us (level)
  Pallas kernels: 39.2 us -> 37.6 us
  waiting for transfers between devices: 26.8 us -> 28.3 us
    pallas_call x2 -> x1, Pallas kernels: 16.2 us -> 14.6 us  [second_call(): pl.pallas_call(second_kernel, in_specs=[pl.BlockSpec(memory_space=pltpu.S...]
    all_gather x1, waiting for transfers between devices: 0.01 us -> 1.49 us  [on_device(): across = lax.all_gather(piece, 'rows', axis=0, tiled=True)]
  transfers between devices with their start and end apart: 20 -> 20, of which waited for: 12 -> 13; matrix products, arithmetic and copies ran while one was open for 0% -> 0% of each run, Pallas kernels for 24% -> 22%
where the time goes in v3:
time: 122 us
  starting transfers between devices  41.7 us (34%)
  Pallas kernels  37.6 us (31%)
  waiting for transfers between devices  28.3 us (23%)
  between operations  14.3 us (12%)
    ppermute x7, starting transfers between devices, along_rows(): return lax.ppermute(array, 'rows', pairs)  28 us
    ppermute x7, waiting for transfers between devices, along_rows(): return lax.ppermute(array, 'rows', pairs)  15.2 us
    pallas_call x1, Pallas kernels, second_call(): pl.pallas_call(second_kernel, in_specs=[pl.BlockSpec(memory_space=pltpu.S...  14.6 us
    ppermute x12, starting transfers between devices, along_y(): lax.ppermute(array, 'cols', [(i, (i + shift) % cols_count) for i in range...  13.6 us
    ppermute x12, waiting for transfers between devices, along_y(): lax.ppermute(array, 'cols', [(i, (i + shift) % cols_count) for i in range...  11.7 us
    pallas_call x1, Pallas kernels, first_call(): pl.pallas_call(first_kernel, out_shape=[square(PW), square(PW), square(PW...  11.5 us
    pallas_call x1, Pallas kernels, update_call(): pl.pallas_call(update_kernel, in_specs=[pl.BlockSpec(memory_space=pltpu.H...  7.12 us
    pallas_call x3, Pallas kernels, choose_call(): pl.pallas_call(body, in_specs=[pl.BlockSpec(memory_space=pltpu.SMEM)] + [...  2.44 us
  transfers between devices with their start and end apart: 20, of which 13 were waited for; matrix products, arithmetic and copies ran while one was open for 0% of the time, Pallas kernels for 22%

profile of v3, /device:TPU:1, one launch (start us, length us, event | category | flops | bytes accessed | tf_op | source)
XLA Modules:
  0.0 122.1 jit_solution(17248080730559770687)
XLA Ops:
  7.2 0.0 all-gather.2.cloned.1.call-start
  7.2 2.0 %pack_messages.1 = (f32[64,512]{1,0:T(8,128)S(1)}, f32[64,512]{1,0:T(8,128)S(1)}, f32[64,512]{1,0:T(8,128)S(1)}, f32[64,512]{1,0:T(8,128)S(1)}, f32[32,512]{1,0:...) custom-call(s32[2]{0:T(128)} %order_ref.7, ...), custom_call_target="tpu_custom_call" | custom-call | bytes 2000000 | tf_op jit(solution)/shard_map/pack_messages/pallas_call | solution.py:355
  9.3 2.2 %collective-permute-start.12 = (f32[64,512]{1,0:T(8,128)S(1)}, f32[64,512]{1,0:T(8,128)S(1)}, u32[]{:S(2)}, u32[]{:S(2)}) collective-permute-start(f32[64,512]{1,0:T(8,128)S(1)} %get-tuple-element.39), channel_id=1, source_target_pairs={{0,1},{1,2},{2,3},{3,0},{4,5},{5,6},{6,7},{7,4},{8,9},{9,10},{10,1... | collective-permute-start | bytes 393224 | tf_op jit(solution)/shard_map/ppermute | solution.py:444
  11.5 2.6 %collective-permute-start.13 = (f32[64,512]{1,0:T(8,128)S(1)}, f32[64,512]{1,0:T(8,128)S(1)}, u32[]{:S(2)}, u32[]{:S(2)}) collective-permute-start(f32[64,512]{1,0:T(8,128)S(1)} %get-tuple-element.40), channel_id=1, source_target_pairs={{0,2},{1,3},{2,0},{3,1},{4,6},{5,7},{6,4},{7,5},{8,10},{9,11},{10,... | collective-permute-start | bytes 393224 | tf_op jit(solution)/shard_map/ppermute | solution.py:444
  14.1 1.1 collective-permute-start.14
  15.2 0.1 collective-permute-done.12.refs_1_
  15.3 4.5 %collective-permute-done.13.refs_2_ = f32[64,512]{1,0:T(8,128)S(1)} collective-permute-done((f32[64,512]{1,0:T(8,128)S(1)}, f32[64,512]{1,0:T(8,128)S(1)}, u32[]{:S(2)}, u32[]{:S(2)}) %collective-permute-start.13) | collective-permute-done | bytes 131104 | tf_op jit(solution)/shard_map/ppermute | solution.py:444
  19.8 0.0 collective-permute-done.14.refs_3_
  19.8 1.3 %choose_pieces.1.refs_0_ = f32[64,512]{1,0:T(8,128)} custom-call(s32[2]{0:T(128)S(1)} %copy-done.1, f32[64,512]{1,0:T(8,128)S(1)} %get-tuple-element.38.refs_0_, f32[64,512]{1,0:T(8,128)S(1)} %collective-permute-done.12.refs_1_, f32[64,512]{1,0:T(8,128)S(1)} %collective-permute-done.13.refs_2_, f32[64,512]{1,0:T(8,128)S(1)} %collective-permute-done.14.refs_3_), custom_call_target="tpu_custom_call" | custom-call | bytes 1000000 | tf_op jit(solution)/shard_map/choose_pieces/pallas_call | solution.py:428
  21.0 0.0 all-gather.2.cloned.1.call-update
  21.1 0.1 collective-permute-start
  21.2 2.1 %collective-permute-start.1 = (f32[32,512]{1,0:T(8,128)S(1)}, f32[32,512]{1,0:T(8,128)S(1)}, u32[]{:S(2)}, u32[]{:S(2)}) collective-permute-start(f32[32,512]{1,0:T(8,128)S(1)} %get-tuple-element.35), channel_id=1, source_target_pairs={{0,2},{1,3},{2,0},{3,1},{4,6},{5,7},{6,4},{7,5},{8,10},{9,11},{10,... | collective-permute-start | bytes 196616 | tf_op jit(solution)/shard_map/ppermute | solution.py:444
  23.3 1.7 %collective-permute-start.2 = (f32[32,512]{1,0:T(8,128)S(1)}, f32[32,512]{1,0:T(8,128)S(1)}, u32[]{:S(2)}, u32[]{:S(2)}) collective-permute-start(f32[32,512]{1,0:T(8,128)S(1)} %get-tuple-element.36), channel_id=1, source_target_pairs={{0,3},{1,0},{2,1},{3,2},{4,7},{5,4},{6,5},{7,6},{8,11},{9,8},{10,9... | collective-permute-start | bytes 196616 | tf_op jit(solution)/shard_map/ppermute | solution.py:444
  24.9 1.2 %collective-permute-done.refs_1_ = f32[32,512]{1,0:T(8,128)S(1)} collective-permute-done((f32[32,512]{1,0:T(8,128)S(1)}, f32[32,512]{1,0:T(8,128)S(1)}, u32[]{:S(2)}, u32[]{:S(2)}) %collective-permute-start) | collective-permute-done | bytes 65568 | tf_op jit(solution)/shard_map/ppermute | solution.py:444
  26.2 0.0 collective-permute-done.1.refs_2_
  26.2 0.6 collective-permute-done.2.refs_3_
  26.8 0.6 choose_shares.1.refs_0_
  27.4 3.6 %collective-permute-start.5 = (f32[64,512]{1,0:T(8,128)S(1)}, f32[64,512]{1,0:T(8,128)S(1)}, u32[]{:S(2)}, u32[]{:S(2)}) collective-permute-start(f32[64,512]{1,0:T(8,128)S(1)} %choose_shares.1.refs_0_), channel_id=1, source_target_pairs={{0,192},{4,196},{8,200},{12,204},{16,208},{20,212},{24,216},{28,22... | collective-permute-start | bytes 393224 | tf_op jit(solution)/shard_map/ppermute | solution.py:453
  31.0 0.5 collective-permute-start.4
  31.5 0.6 collective-permute-start.3
  32.1 2.2 %collective-permute-done.5.refs_3_ = f32[64,512]{1,0:T(8,128)S(1)} collective-permute-done((f32[64,512]{1,0:T(8,128)S(1)}, f32[64,512]{1,0:T(8,128)S(1)}, u32[]{:S(2)}, u32[]{:S(2)}) %collective-permute-start.5) | collective-permute-done | bytes 131104 | tf_op jit(solution)/shard_map/ppermute | solution.py:453
  34.3 2.1 %collective-permute-done.4.refs_2_ = f32[64,512]{1,0:T(8,128)S(1)} collective-permute-done((f32[64,512]{1,0:T(8,128)S(1)}, f32[64,512]{1,0:T(8,128)S(1)}, u32[]{:S(2)}, u32[]{:S(2)}) %collective-permute-start.4) | collective-permute-done | bytes 131104 | tf_op jit(solution)/shard_map/ppermute | solution.py:453
  36.4 1.3 %collective-permute-done.3.refs_1_ = f32[64,512]{1,0:T(8,128)S(1)} collective-permute-done((f32[64,512]{1,0:T(8,128)S(1)}, f32[64,512]{1,0:T(8,128)S(1)}, u32[]{:S(2)}, u32[]{:S(2)}) %collective-permute-start.3) | collective-permute-done | bytes 131104 | tf_op jit(solution)/shard_map/ppermute | solution.py:453
  37.7 0.6 choose_along_x.1
  38.3 3.1 %collective-permute-start.6 = (f32[64,512]{1,0:T(8,128)S(1)}, f32[64,512]{1,0:T(8,128)S(1)}, u32[]{:S(2)}, u32[]{:S(2)}) collective-permute-start(f32[64,512]{1,0:T(8,128)S(1)} %choose_along_x.1), channel_id=1, source_target_pairs={{0,16},{4,20},{8,24},{12,28},{16,0},{20,4},{24,8},{28,12},{32,48},... | collective-permute-start | bytes 393224 | tf_op jit(solution)/shard_map/ppermute | solution.py:453
  41.4 2.4 %collective-permute-done.6 = f32[64,512]{1,0:T(8,128)S(1)} collective-permute-done((f32[64,512]{1,0:T(8,128)S(1)}, f32[64,512]{1,0:T(8,128)S(1)}, u32[]{:S(2)}, u32[]{:S(2)}) %collective-permute-start.6) | collective-permute-done | bytes 131104 | tf_op jit(solution)/shard_map/ppermute | solution.py:453
  43.8 6.3 %collective-permute-start.7 = (f32[64,512]{1,0:T(8,128)S(1)}, f32[64,512]{1,0:T(8,128)S(1)}, u32[]{:S(2)}, u32[]{:S(2)}) collective-permute-start(f32[64,512]{1,0:T(8,128)S(1)} %compare_select_fusion), channel_id=1, source_target_pairs={{0,48},{4,52},{8,56},{12,60},{16,32},{20,36},{24,40},{28,44},{32,1... | collective-permute-start | bytes 393224 | tf_op jit(solution)/shard_map/ppermute | solution.py:453
  50.1 3.8 %collective-permute-done.7 = f32[64,512]{1,0:T(8,128)S(1)} collective-permute-done((f32[64,512]{1,0:T(8,128)S(1)}, f32[64,512]{1,0:T(8,128)S(1)}, u32[]{:S(2)}, u32[]{:S(2)}) %collective-permute-start.7) | collective-permute-done | bytes 131104 | tf_op jit(solution)/shard_map/ppermute | solution.py:453
  53.9 2.2 %collective-permute-start.8 = (f32[64,512]{1,0:T(8,128)S(1)}, f32[64,512]{1,0:T(8,128)S(1)}, u32[]{:S(2)}, u32[]{:S(2)}) collective-permute-start(f32[64,512]{1,0:T(8,128)S(1)} %compare_select_fusion.1), channel_id=1, source_target_pairs={{0,8},{4,12},{8,0},{12,4},{16,24},{20,28},{24,16},{28,20},{32,40},... | collective-permute-start | bytes 393224 | tf_op jit(solution)/shard_map/ppermute | solution.py:453
  56.2 3.1 %collective-permute-done.8 = f32[64,512]{1,0:T(8,128)S(1)} collective-permute-done((f32[64,512]{1,0:T(8,128)S(1)}, f32[64,512]{1,0:T(8,128)S(1)}, u32[]{:S(2)}, u32[]{:S(2)}) %collective-permute-start.8) | collective-permute-done | bytes 131104 | tf_op jit(solution)/shard_map/ppermute | solution.py:453
  59.4 0.9 collective-permute-start.11
  60.2 0.8 collective-permute-start.10
  61.0 0.7 collective-permute-start.9
  61.8 5.2 %collective-permute-done.9 = f32[64,512]{1,0:T(8,128)S(1)} collective-permute-done((f32[64,512]{1,0:T(8,128)S(1)}, f32[64,512]{1,0:T(8,128)S(1)}, u32[]{:S(2)}, u32[]{:S(2)}) %collective-permute-start.9) | collective-permute-done | bytes 131104 | tf_op jit(solution)/shard_map/ppermute | solution.py:444
  67.0 0.0 collective-permute-done.10
  67.1 0.0 copy-start
  67.1 0.0 copy-start.2
  67.1 11.7 %collective-permute-start.15 = (f32[320,512]{1,0:T(8,128)S(1)}, f32[320,512]{1,0:T(8,128)S(1)}, u32[]{:S(2)}, u32[]{:S(2)}) collective-permute-start(f32[320,512]{1,0:T(8,128)S(1)} %slice_dynamic-update-slice_fusion.own_ref), channel_id=1, source_target_pairs={{0,4},{4,0},{8,12},{12,8},{16,20},{20,16},{24,28},{28,24},{32,36},... | collective-permute-start | bytes 1966088 | tf_op jit(solution)/shard_map/ppermute | solution.py:453
  78.8 0.3 collective-permute-start.18
  79.1 0.1 collective-permute-start.17
  79.2 1.1 collective-permute-start.16
  80.3 0.2 collective-permute-done.15.other_ref
  80.5 11.5 %eliminate_first.1 = (f32[256,256]{1,0:T(8,128)S(1)}, f32[256,256]{1,0:T(8,128)S(1)}, f32[256,256]{1,0:T(8,128)S(1)}, f32[512,128]{1,0:T(8,128)S(1)}) custom-call(f32[320,512]{1,0:T(8,128)S(1)} %slice_dynamic-update-slice_fusion.own_ref, f32[320,512]{1,0:T(8,128)S(1)} %collective-permute-done.15.other_ref), custom_call_target="tpu_custom_call" | custom-call | flops 12000000000 | bytes 2000000 | tf_op jit(solution)/shard_map/eliminate_first/pallas_call | solution.py:160
  92.0 0.0 collective-permute-done.17.refs_2_
  92.0 0.0 collective-permute-done.16.refs_1_
  92.0 14.6 %eliminate_second.1 = (f32[256,512]{1,0:T(8,128)}, f32[256,512]{1,0:T(8,128)S(1)}, f32[512,128]{1,0:T(8,128)}, f32[256,128]{1,0:T(8,128)}) custom-call(s32[4]{0:T(128)S(1)} %copy-done.2, f32[64,512]{1,0:T(8,128)} %choose_pieces.1.refs_0_, f32[64,512]{1,0:T(8,128)S(1)} %collective-permute-done.16.refs_1_, f32[64,512]{1,0:T(8,128)S(1)} %collective-permute-done.17.refs_2_, ...), custom_call_target="tpu_custom_call" | custom-call | flops 16000000000 | bytes 4000000 | tf_op jit(solution)/shard_map/eliminate_second/pallas_call | solution.py:217
  106.6 1.5 %all-gather.2.cloned.1.call-done.b_ref = f32[4096,512]{1,0:T(8,128)} async-done(((f32[64,512]{1,0:T(8,128)}), f32[4096,512]{1,0:T(8,128)}) %all-gather.2.cloned.1.call-update) | async-done | bytes 8388624 | tf_op jit(solution)/shard_map/all_gather | solution.py:464
  108.1 7.1 %trailing_update.1 = f32[256,4096]{1,0:T(8,128)} custom-call(f32[256,4096]{1,0:T(8,128)} %k_ref.1, f32[256,512]{1,0:T(8,128)S(1)} %get-tuple-element.54.w_ref, f32[4096,512]{1,0:T(8,128)} %all-gather.2.cloned.1.call-done.b_ref), custom_call_target="tpu_custom_call" | custom-call | flops 3221225472 | bytes 16000000 | tf_op jit(solution)/shard_map/trailing_update/pallas_call | solution.py:275
  (20 shorter events, 0.2 us)
Async XLA Ops:
  7.2 12.6 %copy-start.1 = (s32[2]{0:T(128)S(1)}, s32[2]{0:T(128)}, u32[]{:S(2)}) copy-start(s32[2]{0:T(128)} %order_ref.7) | copy-start | bytes 28
  7.2 100.9 %all-gather.2.cloned.1.call-start = ((), (), s32[]{:S(2)}) async-start(), calls=%async_computation | async-start | bytes 8519680 | tf_op jit(solution)/shard_map/all_gather | solution.py:464
  9.3 6.0 %collective-permute-start.12 = (f32[64,512]{1,0:T(8,128)S(1)}, f32[64,512]{1,0:T(8,128)S(1)}, u32[]{:S(2)}, u32[]{:S(2)}) collective-permute-start(f32[64,512]{1,0:T(8,128)S(1)} %get-tuple-element.39), channel_id=1, source_target_pairs={{0,1},{1,2},{2,3},{3,0},{4,5},{5,6},{6,7},{7,4},{8,9},{9,10},{10,1... | collective-permute-start | bytes 393224 | tf_op jit(solution)/shard_map/ppermute | solution.py:444
  11.5 8.3 %collective-permute-start.13 = (f32[64,512]{1,0:T(8,128)S(1)}, f32[64,512]{1,0:T(8,128)S(1)}, u32[]{:S(2)}, u32[]{:S(2)}) collective-permute-start(f32[64,512]{1,0:T(8,128)S(1)} %get-tuple-element.40), channel_id=1, source_target_pairs={{0,2},{1,3},{2,0},{3,1},{4,6},{5,7},{6,4},{7,5},{8,10},{9,11},{10,... | collective-permute-start | bytes 393224 | tf_op jit(solution)/shard_map/ppermute | solution.py:444
  14.1 5.7 %collective-permute-start.14 = (f32[64,512]{1,0:T(8,128)S(1)}, f32[64,512]{1,0:T(8,128)S(1)}, u32[]{:S(2)}, u32[]{:S(2)}) collective-permute-start(f32[64,512]{1,0:T(8,128)S(1)} %get-tuple-element.41), channel_id=1, source_target_pairs={{0,3},{1,0},{2,1},{3,2},{4,7},{5,4},{6,5},{7,6},{8,11},{9,8},{10,9... | collective-permute-start | bytes 393224 | tf_op jit(solution)/shard_map/ppermute | solution.py:444
  21.1 5.1 %collective-permute-start = (f32[32,512]{1,0:T(8,128)S(1)}, f32[32,512]{1,0:T(8,128)S(1)}, u32[]{:S(2)}, u32[]{:S(2)}) collective-permute-start(f32[32,512]{1,0:T(8,128)S(1)} %get-tuple-element.34), channel_id=1, source_target_pairs={{0,1},{1,2},{2,3},{3,0},{4,5},{5,6},{6,7},{7,4},{8,9},{9,10},{10,1... | collective-permute-start | bytes 196616 | tf_op jit(solution)/shard_map/ppermute | solution.py:444
  21.2 5.0 %collective-permute-start.1 = (f32[32,512]{1,0:T(8,128)S(1)}, f32[32,512]{1,0:T(8,128)S(1)}, u32[]{:S(2)}, u32[]{:S(2)}) collective-permute-start(f32[32,512]{1,0:T(8,128)S(1)} %get-tuple-element.35), channel_id=1, source_target_pairs={{0,2},{1,3},{2,0},{3,1},{4,6},{5,7},{6,4},{7,5},{8,10},{9,11},{10,... | collective-permute-start | bytes 196616 | tf_op jit(solution)/shard_map/ppermute | solution.py:444
  23.3 3.5 %collective-permute-start.2 = (f32[32,512]{1,0:T(8,128)S(1)}, f32[32,512]{1,0:T(8,128)S(1)}, u32[]{:S(2)}, u32[]{:S(2)}) collective-permute-start(f32[32,512]{1,0:T(8,128)S(1)} %get-tuple-element.36), channel_id=1, source_target_pairs={{0,3},{1,0},{2,1},{3,2},{4,7},{5,4},{6,5},{7,6},{8,11},{9,8},{10,9... | collective-permute-start | bytes 196616 | tf_op jit(solution)/shard_map/ppermute | solution.py:444
  27.4 7.0 %collective-permute-start.5 = (f32[64,512]{1,0:T(8,128)S(1)}, f32[64,512]{1,0:T(8,128)S(1)}, u32[]{:S(2)}, u32[]{:S(2)}) collective-permute-start(f32[64,512]{1,0:T(8,128)S(1)} %choose_shares.1.refs_0_), channel_id=1, source_target_pairs={{0,192},{4,196},{8,200},{12,204},{16,208},{20,212},{24,216},{28,22... | collective-permute-start | bytes 393224 | tf_op jit(solution)/shard_map/ppermute | solution.py:453
  31.0 5.4 %collective-permute-start.4 = (f32[64,512]{1,0:T(8,128)S(1)}, f32[64,512]{1,0:T(8,128)S(1)}, u32[]{:S(2)}, u32[]{:S(2)}) collective-permute-start(f32[64,512]{1,0:T(8,128)S(1)} %choose_shares.1.refs_0_), channel_id=1, source_target_pairs={{0,128},{4,132},{8,136},{12,140},{16,144},{20,148},{24,152},{28,15... | collective-permute-start | bytes 393224 | tf_op jit(solution)/shard_map/ppermute | solution.py:453
  31.5 6.2 %collective-permute-start.3 = (f32[64,512]{1,0:T(8,128)S(1)}, f32[64,512]{1,0:T(8,128)S(1)}, u32[]{:S(2)}, u32[]{:S(2)}) collective-permute-start(f32[64,512]{1,0:T(8,128)S(1)} %choose_shares.1.refs_0_), channel_id=1, source_target_pairs={{0,64},{4,68},{8,72},{12,76},{16,80},{20,84},{24,88},{28,92},{32,9... | collective-permute-start | bytes 393224 | tf_op jit(solution)/shard_map/ppermute | solution.py:453
  38.3 5.4 %collective-permute-start.6 = (f32[64,512]{1,0:T(8,128)S(1)}, f32[64,512]{1,0:T(8,128)S(1)}, u32[]{:S(2)}, u32[]{:S(2)}) collective-permute-start(f32[64,512]{1,0:T(8,128)S(1)} %choose_along_x.1), channel_id=1, source_target_pairs={{0,16},{4,20},{8,24},{12,28},{16,0},{20,4},{24,8},{28,12},{32,48},... | collective-permute-start | bytes 393224 | tf_op jit(solution)/shard_map/ppermute | solution.py:453
  43.8 10.1 %collective-permute-start.7 = (f32[64,512]{1,0:T(8,128)S(1)}, f32[64,512]{1,0:T(8,128)S(1)}, u32[]{:S(2)}, u32[]{:S(2)}) collective-permute-start(f32[64,512]{1,0:T(8,128)S(1)} %compare_select_fusion), channel_id=1, source_target_pairs={{0,48},{4,52},{8,56},{12,60},{16,32},{20,36},{24,40},{28,44},{32,1... | collective-permute-start | bytes 393224 | tf_op jit(solution)/shard_map/ppermute | solution.py:453
  53.9 5.4 %collective-permute-start.8 = (f32[64,512]{1,0:T(8,128)S(1)}, f32[64,512]{1,0:T(8,128)S(1)}, u32[]{:S(2)}, u32[]{:S(2)}) collective-permute-start(f32[64,512]{1,0:T(8,128)S(1)} %compare_select_fusion.1), channel_id=1, source_target_pairs={{0,8},{4,12},{8,0},{12,4},{16,24},{20,28},{24,16},{28,20},{32,40},... | collective-permute-start | bytes 393224 | tf_op jit(solution)/shard_map/ppermute | solution.py:453
  59.4 7.6 %collective-permute-start.11 = (f32[64,512]{1,0:T(8,128)S(1)}, f32[64,512]{1,0:T(8,128)S(1)}, u32[]{:S(2)}, u32[]{:S(2)}) collective-permute-start(f32[64,512]{1,0:T(8,128)S(1)} %pad_maximum_fusion), channel_id=1, source_target_pairs={{0,3},{1,0},{2,1},{3,2},{4,7},{5,4},{6,5},{7,6},{8,11},{9,8},{10,9... | collective-permute-start | bytes 393224 | tf_op jit(solution)/shard_map/ppermute | solution.py:444
  60.2 6.7 %collective-permute-start.10 = (f32[64,512]{1,0:T(8,128)S(1)}, f32[64,512]{1,0:T(8,128)S(1)}, u32[]{:S(2)}, u32[]{:S(2)}) collective-permute-start(f32[64,512]{1,0:T(8,128)S(1)} %pad_maximum_fusion), channel_id=1, source_target_pairs={{0,2},{1,3},{2,0},{3,1},{4,6},{5,7},{6,4},{7,5},{8,10},{9,11},{10,... | collective-permute-start | bytes 393224 | tf_op jit(solution)/shard_map/ppermute | solution.py:444
  61.0 5.9 %collective-permute-start.9 = (f32[64,512]{1,0:T(8,128)S(1)}, f32[64,512]{1,0:T(8,128)S(1)}, u32[]{:S(2)}, u32[]{:S(2)}) collective-permute-start(f32[64,512]{1,0:T(8,128)S(1)} %pad_maximum_fusion), channel_id=1, source_target_pairs={{0,1},{1,2},{2,3},{3,0},{4,5},{5,6},{6,7},{7,4},{8,9},{9,10},{10,1... | collective-permute-start | bytes 393224 | tf_op jit(solution)/shard_map/ppermute | solution.py:444
  67.1 24.9 %copy-start = (f32[256,128]{1,0:T(8,128)S(1)}, f32[256,128]{1,0:T(8,128)}, u32[]{:S(2)}) copy-start(f32[256,128]{1,0:T(8,128)} %refs_8_.1) | copy-start | bytes 393220
  67.1 24.9 %copy-start.2 = (s32[4]{0:T(128)S(1)}, s32[4]{0:T(128)}, u32[]{:S(2)}) copy-start(s32[4]{0:T(128)} %block_ref.3) | copy-start | bytes 52
  67.1 13.4 %collective-permute-start.15 = (f32[320,512]{1,0:T(8,128)S(1)}, f32[320,512]{1,0:T(8,128)S(1)}, u32[]{:S(2)}, u32[]{:S(2)}) collective-permute-start(f32[320,512]{1,0:T(8,128)S(1)} %slice_dynamic-update-slice_fusion.own_ref), channel_id=1, source_target_pairs={{0,4},{4,0},{8,12},{12,8},{16,20},{20,16},{24,28},{28,24},{32,36},... | collective-permute-start | bytes 1966088 | tf_op jit(solution)/shard_map/ppermute | solution.py:453
  78.8 13.2 %collective-permute-start.18 = (f32[64,512]{1,0:T(8,128)}, f32[64,512]{1,0:T(8,128)S(1)}, u32[]{:S(2)}, u32[]{:S(2)}) collective-permute-start(f32[64,512]{1,0:T(8,128)} %choose_pieces.1.refs_0_), channel_id=1, source_target_pairs={{0,3},{1,0},{2,1},{3,2},{4,7},{5,4},{6,5},{7,6},{8,11},{9,8},{10,9... | collective-permute-start | bytes 393224 | tf_op jit(solution)/shard_map/ppermute | solution.py:444
  79.1 12.9 %collective-permute-start.17 = (f32[64,512]{1,0:T(8,128)}, f32[64,512]{1,0:T(8,128)S(1)}, u32[]{:S(2)}, u32[]{:S(2)}) collective-permute-start(f32[64,512]{1,0:T(8,128)} %choose_pieces.1.refs_0_), channel_id=1, source_target_pairs={{0,2},{1,3},{2,0},{3,1},{4,6},{5,7},{6,4},{7,5},{8,10},{9,11},{10,... | collective-permute-start | bytes 393224 | tf_op jit(solution)/shard_map/ppermute | solution.py:444
  79.2 12.8 %collective-permute-start.16 = (f32[64,512]{1,0:T(8,128)}, f32[64,512]{1,0:T(8,128)S(1)}, u32[]{:S(2)}, u32[]{:S(2)}) collective-permute-start(f32[64,512]{1,0:T(8,128)} %choose_pieces.1.refs_0_), channel_id=1, source_target_pairs={{0,1},{1,2},{2,3},{3,0},{4,5},{5,6},{6,7},{7,4},{8,9},{9,10},{10,1... | collective-permute-start | bytes 393224 | tf_op jit(solution)/shard_map/ppermute | solution.py:444
Sparse Core Ops, SparseCore 0:
  21.2 86.8 all-gather.1
